TPU v7x, 128 devices: a whole 4x4x4 slice. The times are simulated.
128 devices in a mesh: dp: 2 (over x_hi), seq: 32 (over z, y, core), mp: 2 (over x_lo).
Axes of the slice: x: 4 (x_hi: 2, x_lo: 2; x = x_hi * 2 + x_lo), y: 4, z: 4, core: 2. Of those that a mesh axis runs over, the one named last changes fastest.
Arguments:
- inputs: bfloat16 [2, 4096, 2048], P('dp', 'seq'), may hold values from -6 to 6
- clip_starts: int32 [2, 3], P('dp'), may hold values from 0 to 4064, as said below
- pad_lengths: int32 [2], P('dp'), may hold values from 1 to 64, as said below
- w_query: bfloat16 [2048, 2048], P(('dp', 'seq'), 'mp'), may hold values from -0.125 to 0.125
- w_key: bfloat16 [2048, 2048], P(('dp', 'seq'), 'mp'), may hold values from -0.125 to 0.125
- w_value: bfloat16 [2048, 2048], P(('dp', 'seq'), 'mp'), may hold values from -0.125 to 0.125
- w_out: bfloat16 [2048, 2048], P('mp', ('dp', 'seq')), may hold values from -0.75 to 0.75
- w_up: bfloat16 [2048, 8192], P(('dp', 'seq'), 'mp'), may hold values from -0.125 to 0.125
- w_down: bfloat16 [8192, 2048], P('mp', ('dp', 'seq')), may hold values from -0.0625 to 0.0625
- gain_first: bfloat16 [2048], P(('dp', 'seq')), may hold values from 0.099609375 to 1.8984375
- gain_second: bfloat16 [2048], P(('dp', 'seq')), may hold values from 0.099609375 to 1.8984375
- cotangent: bfloat16 [2, 4096, 2048], P('dp', 'seq'), may hold values from -6 to 6
Outputs:
- output: bfloat16 [2, 4096, 2048], P('dp', 'seq')
- grad_input: float32 [2, 4096, 2048], P('dp', 'seq')
- grad_w_query: float32 [2048, 2048], P(('dp', 'seq'), 'mp')
- grad_w_key: float32 [2048, 2048], P(('dp', 'seq'), 'mp')
- grad_w_value: float32 [2048, 2048], P(('dp', 'seq'), 'mp')
- grad_w_out: float32 [2048, 2048], P('mp', ('dp', 'seq'))
- grad_w_up: float32 [2048, 8192], P(('dp', 'seq'), 'mp')
- grad_w_down: float32 [8192, 2048], P('mp', ('dp', 'seq'))
- grad_gain_first: float32 [2048], P(('dp', 'seq'))
- grad_gain_second: float32 [2048], P(('dp', 'seq'))
Inputs may be any that keep to these rules, and one draw needn't show every extreme that they name: `clip_starts`: each row rises strictly from 0 and every start is a multiple of 32; a clip runs from its start to the next start or to the end of the sequence; every clip but the second-to-last holds 1 to 3 frames of 32 tokens, and the second-to-last takes the rest of the sequence. `pad_lengths`: padding tokens are the last ones of their sequence.
All inputs are finite; a program needn't handle non-finite values.
Results may differ from a plain program's by a relative error of at most 0.017.
Values may be sent and summed in bfloat16 or wider, within the bound.
A program may use at most 640 MiB of HBM per device.

v0:
```python
import jax
import jax.numpy as jnp
from jax import lax
from jax.sharding import Mesh
from jax.sharding import PartitionSpec as P

HD = 128
FRAME = 32
SEQ = ("seq_0", "seq_1", "seq_2")
DP_SEQ = ("dp", "seq_0", "seq_1", "seq_2")


epsilon = 1e-05


def from_everyone(value, axis):
    copies = jnp.broadcast_to(value, (lax.axis_size(axis), *value.shape))
    return lax.all_to_all(copies, axis, split_axis=0, concat_axis=0, tiled=True)


def of_everyone(value, axis):
    everything = from_everyone(value, axis)
    return jnp.sum(everything, axis=0)


def turned_gather(arrays, axis, dims):
    turned = [jnp.moveaxis(a, dim, 0) for a, dim in zip(arrays, dims)]
    both = jnp.concatenate([t.reshape(len(t), -1) for t in turned], axis=1)
    filled, at, done = (lax.all_gather(both, axis, axis=0, tiled=True), 0, [])
    for t, dim in zip(turned, dims):
        section = filled[:, at : at + t[0].size].reshape(-1, *t.shape[1:])
        done.append(jnp.moveaxis(section, 0, dim))
        at += t[0].size
    return tuple(done)


def split_up(value, dim, devices):
    before, after = (value.shape[:dim], value.shape[dim + 1 :])
    return jnp.moveaxis(value.reshape(*before, devices, -1, *after), dim, 0)


def summed_rows(value, chips, core, dim):
    sizes = (lax.axis_size(chips), lax.axis_size(core))
    parts = split_up(value, dim, sizes[0] * sizes[1])
    inside = parts.shape[1:]
    parts = parts.reshape(*sizes, *inside).swapaxes(0, 1).reshape(-1, *inside)
    parts = lax.psum_scatter(parts, core, scatter_dimension=0, tiled=True)
    return lax.psum_scatter(parts, chips, scatter_dimension=0, tiled=True)[0]


def sent_together(arrays, axis, dim, along):
    both = jnp.concatenate(arrays, axis=along)
    filled, at, done = (lax.all_gather(both, axis, axis=dim, tiled=True), 0, [])
    for a in arrays:
        done.append(lax.slice_in_dim(filled, at, at + a.shape[along], axis=along))
        at += a.shape[along]
    return tuple(done)


def in_one_piece(arrays, axis, dim, along):
    both = jnp.concatenate(arrays, axis=along)
    filled, at, done = (lax.psum_scatter(both, axis, scatter_dimension=dim, tiled=True), 0, [])
    for a in arrays:
        done.append(lax.slice_in_dim(filled, at, at + a.shape[along], axis=along))
        at += a.shape[along]
    return tuple(done)


def normed(value, gain):
    centre = value - jnp.mean(value, -1, keepdims=True)
    spread = jnp.mean(centre * centre, -1, keepdims=True)
    return centre * lax.rsqrt(spread + epsilon) * gain


def rotary(value, places, direction):
    half_dim = value.shape[-1] // 2
    frequency = 10000.0 ** (-2.0 * jnp.arange(half_dim, dtype=jnp.float32) / value.shape[-1])
    angles = places.astype(jnp.float32)[:, None] * frequency[None, :]
    cosine = jnp.cos(angles)[:, None, :]
    sine = jnp.sin(angles)[:, None, :]
    first = value[..., :half_dim]
    second = value[..., half_dim:]
    return jnp.concatenate(
        [first * cosine - direction * second * sine, direction * first * sine + second * cosine], -1
    )


def layout(starts, padding, length):
    places = jnp.arange(length, dtype=jnp.int32)
    opened = starts[None, :] <= places[:, None]
    segment = jnp.sum(opened.astype(jnp.int32), -1) - 1
    clip_begin = jnp.max(jnp.where(opened, starts[None, :], 0), -1)
    position = places - clip_begin
    frame_no = position // FRAME
    living = places < length - padding
    return (places, segment, position, frame_no, living)


def visible(query_info, key_info):
    query_place, query_segment, query_frame, query_living = query_info
    key_place, key_segment, key_frame, key_living = key_info
    same = query_segment[:, None] == key_segment[None, :]
    earlier = key_frame[None, :] <= query_frame[:, None]
    both = query_living[:, None] & key_living[None, :]
    return (query_place[:, None] == key_place[None, :]) | same & earlier & both


def gelu_exact(value):
    return jax.nn.gelu(value, approximate=False)


def contract_rows(left, right):
    return lax.dot_general(
        left, right, (((0,), (0,)), ((), ())), preferred_element_type=jnp.float32
    )


def contract_cols(left, right):
    return lax.dot_general(
        left, right, (((1,), (1,)), ((), ())), preferred_element_type=jnp.float32
    )


def join_model(term):
    return of_everyone(term, "mp")


def join_grads(term):
    return of_everyone(term, "mp")


def local(
    inputs,
    clip_starts,
    pad_lengths,
    w_query,
    w_key,
    w_value,
    w_out,
    w_up,
    w_down,
    gain_first,
    gain_second,
    cotangent,
):
    local_rows = inputs.shape[1]
    length = local_rows * lax.axis_size(SEQ)
    score_scale = HD ** (-0.5)
    places, segment, position, frame_no, living = layout(clip_starts[0], pad_lengths[0], length)
    offset = lax.axis_index(SEQ) * local_rows

    def own(whole):
        return lax.dynamic_slice_in_dim(whole, offset, local_rows)

    all_info = (places, segment, frame_no, living)
    own_info = (own(places), own(segment), own(frame_no), own(living))
    mask = visible(own_info, all_info)
    own_position = own(position)
    gathered = turned_gather(
        (w_query, w_key, w_value, w_out, w_up, w_down, gain_first, gain_second),
        DP_SEQ,
        (0, 0, 0, 1, 0, 1, 0, 0),
    )
    query_full, key_full, value_full, out_full, up_full, down_full, gain_one, gain_two = gathered
    heads_here = query_full.shape[1] // HD
    input_wide = inputs[0].astype(jnp.float32)
    normed_one = normed(input_wide, gain_one.astype(jnp.float32)).astype(jnp.bfloat16)

    def project(weight):
        return jnp.dot(normed_one, weight, preferred_element_type=jnp.float32).reshape(
            local_rows, heads_here, HD
        )

    queries = rotary(project(query_full), own_position, 1.0).astype(jnp.bfloat16)
    keys_own = rotary(project(key_full), own_position, 1.0).astype(jnp.bfloat16)
    values_own = project(value_full).astype(jnp.bfloat16)
    both_all = lax.all_gather(jnp.stack([keys_own, values_own], 1), SEQ, axis=0, tiled=True)
    keys_all = both_all[:, 0]
    values_all = both_all[:, 1]

    def scores():
        raw = (
            jnp.einsum("qhd,khd->hqk", queries, keys_all, preferred_element_type=jnp.float32)
            * score_scale
        )
        return jnp.where(mask[None], raw, -1e30)

    raw_scores = scores()
    largest = jnp.max(raw_scores, -1, keepdims=True)
    expo = jnp.exp(raw_scores - largest)
    total = jnp.sum(expo, -1, keepdims=True)
    probs = expo / total
    log_total = largest + jnp.log(total)
    mixed = jnp.einsum(
        "hqk,khd->qhd", probs.astype(jnp.bfloat16), values_all, preferred_element_type=jnp.float32
    )
    mixed = mixed.reshape(local_rows, heads_here * HD).astype(jnp.bfloat16)
    middle = input_wide + join_model(jnp.dot(mixed, out_full, preferred_element_type=jnp.float32))
    normed_two = normed(middle, gain_two.astype(jnp.float32)).astype(jnp.bfloat16)
    hidden = jnp.dot(normed_two, up_full, preferred_element_type=jnp.float32)
    active = gelu_exact(hidden).astype(jnp.bfloat16)
    output = (
        middle + join_model(jnp.dot(active, down_full, preferred_element_type=jnp.float32))
    ).astype(jnp.bfloat16)
    again = turned_gather(
        (w_query, w_key, w_value, w_out, w_up, w_down, gain_first, gain_second),
        DP_SEQ,
        (0, 0, 0, 1, 0, 1, 0, 0),
    )
    query_back, key_back, value_back, out_back, up_back, down_back, gain_one_back, gain_two_back = (
        again
    )
    incoming = cotangent[0]
    grad_down = contract_rows(active, incoming)
    grad_active = contract_cols(incoming, down_back)
    unused_value, gelu_pull = jax.vjp(gelu_exact, hidden)
    grad_hidden = gelu_pull(grad_active)[0].astype(jnp.bfloat16)
    grad_up = contract_rows(normed_two, grad_hidden)
    grad_normed_two = join_grads(contract_cols(grad_hidden, up_back))
    unused_two, norm_pull_two = jax.vjp(normed, middle, gain_two_back.astype(jnp.float32))
    grad_middle_norm, grad_gain_two = norm_pull_two(grad_normed_two)
    grad_middle = incoming.astype(jnp.float32) + grad_middle_norm
    feed_grads = (
        summed_rows(grad_up, ("dp", "seq_0", "seq_1"), "seq_2", 0),
        summed_rows(grad_down, ("dp", "seq_0", "seq_1"), "seq_2", 1),
        summed_rows(grad_gain_two, ("dp", "seq_0", "seq_1"), "seq_2", 0),
    )
    grad_branch = grad_middle.astype(jnp.bfloat16)
    grad_out = contract_rows(mixed, grad_branch)
    grad_mixed = (
        contract_cols(grad_branch, out_back)
        .astype(jnp.bfloat16)
        .reshape(local_rows, heads_here, HD)
    )
    probs_again = jnp.exp(scores() - log_total)
    grad_probs = jnp.einsum(
        "qhd,khd->hqk", grad_mixed, values_all, preferred_element_type=jnp.float32
    )
    inner = jnp.sum(probs_again * grad_probs, -1, keepdims=True)
    grad_scores = (probs_again * (grad_probs - inner)).astype(jnp.bfloat16)
    grad_queries = (
        jnp.einsum("hqk,khd->qhd", grad_scores, keys_all, preferred_element_type=jnp.float32)
        * score_scale
    )
    queries_all, grad_mixed_all = sent_together((queries, grad_mixed), SEQ, 0, 1)
    log_all, inner_all = sent_together((log_total, inner), SEQ, 1, 0)
    back_mask = visible(all_info, own_info)
    raw_back = (
        jnp.einsum("qhd,khd->hqk", queries_all, keys_own, preferred_element_type=jnp.float32)
        * score_scale
    )
    raw_back = jnp.where(back_mask[None], raw_back, -1e30)
    probs_back = jnp.exp(raw_back - log_all)
    grad_probs_back = jnp.einsum(
        "qhd,khd->hqk", grad_mixed_all, values_own, preferred_element_type=jnp.float32
    )
    grad_scores_back = (probs_back * (grad_probs_back - inner_all)).astype(jnp.bfloat16)
    grad_keys_own = (
        jnp.einsum(
            "hqk,qhd->khd", grad_scores_back, queries_all, preferred_element_type=jnp.float32
        )
        * score_scale
    )
    grad_values_own = jnp.einsum(
        "hqk,qhd->khd",
        probs_back.astype(jnp.bfloat16),
        grad_mixed_all,
        preferred_element_type=jnp.float32,
    )
    grad_query_lin = (
        rotary(grad_queries, own_position, -1.0)
        .reshape(local_rows, heads_here * HD)
        .astype(jnp.bfloat16)
    )
    grad_key_lin = (
        rotary(grad_keys_own, own_position, -1.0)
        .reshape(local_rows, heads_here * HD)
        .astype(jnp.bfloat16)
    )
    grad_value_lin = grad_values_own.reshape(local_rows, heads_here * HD).astype(jnp.bfloat16)
    grad_w_query = contract_rows(normed_one, grad_query_lin)
    grad_w_key = contract_rows(normed_one, grad_key_lin)
    grad_w_value = contract_rows(normed_one, grad_value_lin)
    partial_one = (
        contract_cols(grad_query_lin, query_back)
        + contract_cols(grad_key_lin, key_back)
        + contract_cols(grad_value_lin, value_back)
    )
    grad_normed_one = join_grads(partial_one)
    unused_one, norm_pull_one = jax.vjp(normed, input_wide, gain_one_back.astype(jnp.float32))
    grad_input_norm, grad_gain_one = norm_pull_one(grad_normed_one)
    grad_input = grad_middle + grad_input_norm
    mixer_grads = (
        *in_one_piece((grad_w_query, grad_w_key, grad_w_value), DP_SEQ, 0, 1),
        lax.psum_scatter(grad_out, DP_SEQ, scatter_dimension=1, tiled=True),
        lax.psum_scatter(grad_gain_one, DP_SEQ, scatter_dimension=0, tiled=True),
    )
    return (
        output[None],
        grad_input[None],
        mixer_grads[0],
        mixer_grads[1],
        mixer_grads[2],
        mixer_grads[3],
        feed_grads[0],
        feed_grads[1],
        mixer_grads[4],
        feed_grads[2],
    )


def solution(mesh):
    split = Mesh(
        mesh.devices.reshape(mesh.shape["dp"], 4, 4, 2, mesh.shape["mp"]),
        ("dp", "seq_0", "seq_1", "seq_2", "mp"),
    )
    placed = (
        P("dp", SEQ, None),
        P("dp", None),
        P("dp"),
        P(DP_SEQ, "mp"),
        P(DP_SEQ, "mp"),
        P(DP_SEQ, "mp"),
        P("mp", DP_SEQ),
        P(DP_SEQ, "mp"),
        P("mp", DP_SEQ),
        P(DP_SEQ),
        P(DP_SEQ),
        P("dp", SEQ, None),
    )
    return jax.shard_map(
        local,
        mesh=split,
        in_specs=placed,
        out_specs=(
            P("dp", SEQ, None),
            P("dp", SEQ, None),
            P(DP_SEQ, "mp"),
            P(DP_SEQ, "mp"),
            P(DP_SEQ, "mp"),
            P("mp", DP_SEQ),
            P(DP_SEQ, "mp"),
            P("mp", DP_SEQ),
            P(DP_SEQ),
            P(DP_SEQ),
        ),
        check_vma=False,
    )
```

profile of v0, /device:TPU:1, one launch (start us, length us, event | category | flops | bytes accessed | tf_op | source)
XLA Modules:
  0.0 1778.5 jit_solution(173769730868331371)
XLA Ops:
  12.5 215.9 %all-gather.4.cloned.1.call-done = bf16[2048,12290]{1,0:T(8,128)(2,1)} async-done(((bf16[32,12290]{1,0:T(8,128)(2,1)}), bf16[2048,12290]{1,0:T(8,128)(2,1)}) %all-gather.4.cloned.1.call-update) | async-done | bytes 50339856 | tf_op jit(solution)/shard_map/all_gather | solution.py:29
  271.2 76.8 %all-gather.6.cloned.1.call-done = bf16[4096,2,8,128]{0,3,2,1:T(8,128)(2,1)} async-done(((bf16[128,2,8,128]{0,3,2,1:T(8,128)(2,1)}), bf16[4096,2,8,128]{0,3,2,1:T(8,128)(2,1)}) %all-gather.6.cloned.1.call-update) | async-done | bytes 16777232 | tf_op jit(solution)/shard_map/all_gather | solution.py:177
  365.1 10.9 fusion.65
  380.1 28.4 %all_to_all.20 = f32[2,128,2048]{2,1,0:T(8,128)} all-to-all(f32[2,128,2048]{2,1,0:T(8,128)S(1)} %broadcast_in_dim.61), channel_id=1, replica_groups=mesh['dp'=2,'seq_0'=4,'seq_1'=4,'seq_2'=2,'mp'=2] {'mp'}, dimensions={0} | all-to-all | bytes 4194304 | tf_op jit(solution)/shard_map/all_to_all | solution.py:18
  419.4 10.8 add_convert_fusion
  440.1 27.2 %all_to_all.21 = f32[2,128,2048]{2,1,0:T(8,128)} all-to-all(f32[2,128,2048]{2,1,0:T(8,128)S(1)} %broadcast_in_dim.63), channel_id=1, replica_groups=mesh['dp'=2,'seq_0'=4,'seq_1'=4,'seq_2'=2,'mp'=2] {'mp'}, dimensions={0} | all-to-all | bytes 4194304 | tf_op jit(solution)/shard_map/all_to_all | solution.py:18
  475.6 15.9 convolution_bitcast_fusion
  491.4 38.6 %reshape.811 = f32[32,2,4096,32]{2,1,0,3:T(2,128)} reshape(f32[64,4096,32]{1,0,2:T(8,128)} %convolution_bitcast_fusion) | data formatting | bytes 67108864 | tf_op jit(solution)/shard_map/reshape | solution.py:46
  530.1 32.2 %copy.183 = f32[2,32,4096,32]{2,3,1,0:T(8,128)} copy(f32[2,32,4096,32]{2,0,1,3:T(2,128)} %bitcast.197) | data formatting | bytes 67108864 | tf_op jit(solution)/shard_map/transpose | solution.py:46
  563.5 15.3 convolution_bitcast_fusion.1
  578.8 30.6 %copy.180 = f32[2,32,32,4096]{3,2,1,0:T(8,128)} copy(f32[2,32,32,4096]{3,2,0,1:T(8,128)} %convolution_bitcast_fusion.1) | data formatting | bytes 67108864 | tf_op jit(solution)/shard_map/transpose | solution.py:46
  614.3 15.9 multiply_reduce_fusion
  630.2 28.7 %all_gather.16 = f32[16,4096,1]{1,0,2:T(8,128)S(1)} all-gather(f32[16,128,1]{1,0,2:T(8,128)S(1)} %pad_maximum_fusion.3), channel_id=1, replica_groups=mesh['dp'=2,'seq_0'=4,'seq_1'=4,'seq_2'=2,'mp'=2] {'seq_0','seq_1','seq_2'}, dimensions={1}, use_global_device_ids=true | all-gather | bytes 270336 | tf_op jit(solution)/shard_map/all_gather | solution.py:53
  659.0 17.6 fusion.61
  676.6 12.0 fusion.106
  688.6 14.9 multiply_convert_fusion
  736.9 24.7 %copy.199 = f32[2048,3072]{1,0:T(8,128)} copy(f32[2048,3072]{0,1:T(8,128)} %pad_maximum_fusion) | data formatting | bytes 50331648
  770.3 13.6 fusion.3
  802.5 12.9 all-to-all-done.1
  827.6 165.0 %all-reduce.1 = f32[32,32]{0,1:T(8,128)S(1)} all-reduce(f32[32,32]{0,1:T(8,128)S(1)} %copy.202), channel_id=10, replica_groups=mesh['dp'=2,'seq_0'=4,'seq_1'=4,'seq_2'=2,'mp'=2] {'dp','seq_0','seq_1'}, use_global_device_ids=true, to_apply=%region_27.28.clone | all-reduce | flops 1024 | bytes 8192
  996.7 191.7 %all-reduce = f32[2048]{0:T(1024)S(1)} all-reduce(f32[2048]{0:T(1024)S(1)} %get-tuple-element.74), channel_id=8, replica_groups=mesh['dp'=2,'seq_0'=4,'seq_1'=4,'seq_2'=2,'mp'=2] {'dp','seq_0','seq_1',..., use_global_device_ids=true, to_apply=%region_24.25.clone | all-reduce | flops 2048 | bytes 16384
  1194.3 142.4 %reduce-scatter.13.cloned.1.call-done = f32[1024,32]{0,1:T(8,128)} async-done(((f32[1024,2048]{0,1:T(8,128)}), f32[1024,32]{0,1:T(8,128)}) %reduce-scatter.13.cloned.1.call-update) | async-done | bytes 131088 | tf_op jit(solution)/shard_map/reduce_scatter | solution.py:295
  1336.7 209.7 %reduce-scatter.21.cloned.1.call-done = f32[1,4096,32]{1,2,0:T(8,128)} async-done(((f32[32,4096,32]{1,2,0:T(8,128)}), f32[1,4096,32]{1,2,0:T(8,128)}) %reduce-scatter.21.cloned.1.call-update) | async-done | bytes 524304 | tf_op jit(solution)/shard_map/reduce_scatter | solution.py:48
  1546.4 224.8 %reduce-scatter.17.cloned.1.call-done = f32[1,32,4096]{2,1,0:T(8,128)} async-done(((f32[32,32,4096]{2,1,0:T(8,128)}), f32[1,32,4096]{2,1,0:T(8,128)}) %reduce-scatter.17.cloned.1.call-update) | async-done | bytes 524304 | tf_op jit(solution)/shard_map/reduce_scatter | solution.py:48
  (258 shorter events, 185.1 us)
Async XLA Ops:
  7.2 221.3 %all-gather.4.cloned.1.call-start = ((), (), s32[]{:S(2)}) async-start(), calls=%async_computation.11 | async-start | bytes 51650560 | tf_op jit(solution)/shard_map/all_gather | solution.py:29
  10.9 337.2 %all-gather.6.cloned.1.call-start = ((), (), s32[]{:S(2)}) async-start(), calls=%async_computation.12 | async-start | bytes 17301504 | tf_op jit(solution)/shard_map/all_gather | solution.py:177
  11.1 259.1 %copy-start.36 = (s32[4096]{0:T(1024)}, s32[4096]{0:T(1024)S(1)}, u32[]{:S(2)}) copy-start(s32[4096]{0:T(1024)S(1)} %get-tuple-element.105) | copy-start | bytes 49156
  11.4 252.5 %copy-start.41 = (f32[128]{0:T(128)}, f32[128]{0:T(128)S(1)}, u32[]{:S(2)}) copy-start(f32[128]{0:T(128)S(1)} %broadcast_multiply_fusion.2) | copy-start | bytes 1540
  11.7 225.9 %copy-start.68 = (f32[128]{0:T(128)}, f32[128]{0:T(128)S(1)}, u32[]{:S(2)}) copy-start(f32[128]{0:T(128)S(1)} %fusion.71) | copy-start | bytes 1540
  11.7 252.2 %copy-start.47 = (f32[128]{0:T(128)}, f32[128]{0:T(128)S(1)}, u32[]{:S(2)}) copy-start(f32[128]{0:T(128)S(1)} %fusion.112) | copy-start | bytes 1540
  12.5 255.0 %copy-start.29 = (f32[128,64]{0,1:T(8,128)}, f32[128,64]{0,1:T(8,128)S(1)}, u32[]{:S(2)}) copy-start(f32[128,64]{0,1:T(8,128)S(1)} %get-tuple-element.109) | copy-start | bytes 98308
  252.3 217.3 %copy-start.34 = (f32[2048]{0:T(1024)}, f32[2048]{0:T(1024)S(1)}, u32[]{:S(2)}) copy-start(f32[2048]{0:T(1024)S(1)} %get-tuple-element.70) | copy-start | bytes 24580
  267.6 80.4 %copy-start.17 = (bf16[128,8,64]{0,2,1:T(8,128)(2,1)}, bf16[128,8,64]{0,2,1:T(8,128)(2,1)S(1)}, u32[]{:S(2)}) copy-start(bf16[128,8,64]{0,2,1:T(8,128)(2,1)S(1)} %get-tuple-element.103) | copy-start | bytes 393220
  267.7 80.4 %copy-start.19 = (bf16[128,8,64]{0,2,1:T(8,128)(2,1)}, bf16[128,8,64]{0,2,1:T(8,128)(2,1)S(1)}, u32[]{:S(2)}) copy-start(bf16[128,8,64]{0,2,1:T(8,128)(2,1)S(1)} %get-tuple-element.104) | copy-start | bytes 393220
  267.7 86.7 %copy-start.21 = (bf16[128,8,64]{0,2,1:T(8,128)(2,1)}, bf16[128,8,64]{0,2,1:T(8,128)(2,1)S(1)}, u32[]{:S(2)}) copy-start(bf16[128,8,64]{0,2,1:T(8,128)(2,1)S(1)} %get-tuple-element.92) | copy-start | bytes 393220
  267.7 86.7 %copy-start.23 = (bf16[128,8,64]{0,2,1:T(8,128)(2,1)}, bf16[128,8,64]{0,2,1:T(8,128)(2,1)S(1)}, u32[]{:S(2)}) copy-start(bf16[128,8,64]{0,2,1:T(8,128)(2,1)S(1)} %get-tuple-element.93) | copy-start | bytes 393220
  269.0 407.5 %all-gather.8.cloned.1.call-start = ((), (), s32[]{:S(2)}) async-start(), calls=%async_computation.13 | async-start | bytes 17301504 | tf_op jit(solution)/shard_map/all_gather | solution.py:53
  269.4 78.6 %copy-start.59 = (s32[128]{0:T(128)}, s32[128]{0:T(128)S(1)}, u32[]{:S(2)}) copy-start(s32[128]{0:T(128)S(1)} %dynamic_slice.18) | copy-start | bytes 1540
  271.2 93.9 %copy-start.8 = (pred[128,4096]{1,0:T(8,128)(4,1)}, pred[128,4096]{1,0:T(8,128)(4,1)S(1)}, u32[]{:S(2)}) copy-start(pred[128,4096]{1,0:T(8,128)(4,1)S(1)} %fusion.49) | copy-start | bytes 1572868
  474.8 294.2 %reduce-scatter.19.cloned.1.call-start = ((), (), s32[]{:S(2)}) async-start(), calls=%async_computation.17 | async-start | bytes 50331648 | tf_op jit(solution)/shard_map/reduce_scatter | solution.py:47
  562.3 207.5 %reduce-scatter.15.cloned.1.call-start = ((), (), s32[]{:S(2)}) async-start(), calls=%async_computation.15 | async-start | bytes 50331648 | tf_op jit(solution)/shard_map/reduce_scatter | solution.py:47
  609.5 217.3 %reduce-scatter.25.cloned.1.call-start = ((), (), s32[]{:S(2)}) async-start(), calls=%async_computation.20 | async-start | bytes 49152
  658.9 533.6 %reduce-scatter.23.cloned.1.call-start = ((), (), s32[]{:S(2)}) async-start(), calls=%async_computation.19 | async-start | bytes 25559040
  761.6 575.0 %reduce-scatter.13.cloned.1.call-start = ((), (), s32[]{:S(2)}) async-start(), calls=%async_computation.14 | async-start | bytes 8519680 | tf_op jit(solution)/shard_map/reduce_scatter | solution.py:295
  768.9 777.5 %reduce-scatter.21.cloned.1.call-start = ((), (), s32[]{:S(2)}) async-start(), calls=%async_computation.18 | async-start | bytes 17301504 | tf_op jit(solution)/shard_map/reduce_scatter | solution.py:48
  769.7 1001.5 %reduce-scatter.17.cloned.1.call-start = ((), (), s32[]{:S(2)}) async-start(), calls=%async_computation.16 | async-start | bytes 17301504 | tf_op jit(solution)/shard_map/reduce_scatter | solution.py:48
  785.5 29.9 %all-to-all-start.1 = ((f32[2,128,2048]{2,1,0:T(8,128)}), f32[2,128,2048]{2,1,0:T(8,128)}, u32[]{:S(2)}, u32[]{:S(2)}) async-start(f32[2,128,2048]{2,1,0:T(8,128)} %broadcast_in_dim.62), calls=%async_computation.1 | async-start | bytes 4194304 | tf_op jit(solution)/shard_map/all_to_all | solution.py:18
  817.0 176.9 %all-to-all-start.3 = ((f32[2,128,2048]{2,1,0:T(8,128)}), f32[2,128,2048]{2,1,0:T(8,128)}, u32[]{:S(2)}, u32[]{:S(2)}) async-start(f32[2,128,2048]{2,1,0:T(8,128)} %broadcast_in_dim.75), calls=%async_computation.3 | async-start | bytes 4194304 | tf_op jit(solution)/shard_map/all_to_all | solution.py:18
  (61 other events, 729.2 us)
Sparse Core Ops, SparseCore 0:
  11.8 216.5 all-gather.3
  269.2 78.8 all-gather.5
  474.9 82.9 all-gather.7
  562.4 50.5 reduce-scatter.18
  615.2 49.2 reduce-scatter.14
  667.2 11.5 reduce-scatter.24
  761.8 234.0 reduce-scatter.22
  999.0 337.6 reduce-scatter.12
  1339.8 206.5 reduce-scatter.20
  1549.4 221.7 reduce-scatter.16
where the time goes:
time: 1810 us; the launch traced here: 1780 us
  waiting for transfers between devices  884 us (49%)
  blocking collectives  441 us (24%)
  matrix products  206 us (11%)
  local copies, waits for them, and re-layouts  181 us (10%)
  other arithmetic  38.2 us (2%)
    reduce_scatter x2, waiting for transfers between devices, summed_rows(): return lax.psum_scatter(parts, chips, scatter_dimension=0, tiled=True)[0]  435 us
    unnamed x2, blocking collectives  357 us
    all_gather x1, waiting for transfers between devices, turned_gather(): filled, at, done = (lax.all_gather(both, axis, axis=0, tiled=True), 0, [])  216 us
    reduce_scatter x1, waiting for transfers between devices, local(): lax.psum_scatter(grad_out, DP_SEQ, scatter_dimension=1, tiled=True)  142 us
    all_gather x1, waiting for transfers between devices, local(): lax.all_gather(jnp.stack([keys_own, values_own], 1), SEQ, axis=0, tiled=T...  76.8 us
    transpose x2, local copies, waits for them, and re-layouts, summed_rows(): parts = parts.reshape(*sizes, *inside).swapaxes(0, 1).reshape(-1, *inside)  62.8 us
    all_to_all x2, blocking collectives, from_everyone(): return lax.all_to_all(copies, axis, split_axis=0, concat_axis=0, tiled=True)  55.6 us
    dot_general x6, matrix products, contract_rows(): lax.dot_general(left, right, (((0,), (0,)), ((), ())), preferred_element_...  40.9 us
  transfers between devices with their start and end apart: 12, of which 6 were waited for; matrix products, arithmetic and copies ran while one was open for 17% of the time, Pallas kernels for 0%

commit v1 on v0

v1 whole, which is shorter than its diff:
```python
import functools

import jax
import jax.numpy as jnp
from jax import lax
from jax.experimental import pallas as pl
from jax.experimental.pallas import tpu as pltpu
from jax.sharding import Mesh
from jax.sharding import PartitionSpec as P

MESH = pl.DeviceIdType.MESH
HD = 128
FRAME = 32
LEN = 4096
D = 2048
ROWS = 128
BLOCK = 256
ZY = ("z", "y")
epsilon = 1e-05
scale = HD**-0.5
f32 = jnp.float32
bf16 = jnp.bfloat16


def params(collective_id=None, vmem=48, **kw):
    if collective_id is not None:
        kw = dict(collective_id=collective_id, has_side_effects=True, **kw)
    return pltpu.CompilerParams(vmem_limit_bytes=vmem * 2**20, **kw)


def vmem_specs(n):
    return [pl.BlockSpec(memory_space=pltpu.VMEM)] * n


def greet(peers):
    barrier = pltpu.get_barrier_semaphore()
    for peer in peers:
        pl.semaphore_signal(barrier, inc=1, device_id=peer, device_id_type=MESH)
    pl.semaphore_wait(barrier, len(peers))


def remote(src, dst, send, recv, peer):
    return pltpu.make_async_remote_copy(
        src_ref=src, dst_ref=dst, send_sem=send, recv_sem=recv, device_id=peer, device_id_type=MESH
    )


def quarter_kernel(count, *refs):
    srcs, dsts = refs[:count], refs[count : 2 * count]
    send, recv = refs[2 * count :]
    d, c = lax.axis_index("dp"), lax.axis_index("c")
    me = 2 * d + c
    others = [(d, 1 - c), (1 - d, c), (1 - d, 1 - c)]
    peers = [{"dp": a, "c": b} for a, b in others]
    greet(peers)
    out = []
    for k, (a, b) in enumerate(others):
        for i in range(count):
            copy = remote(srcs[i].at[2 * a + b], dsts[i].at[me], send.at[k, i], recv.at[k, i], peers[k])
            copy.start()
            out.append(copy)
    for i in range(count):
        dsts[i][me] = srcs[i][me]
    for copy in out:
        copy.wait()


def swap_quarters(collective_id, *arrays):
    n = len(arrays)
    return pl.pallas_call(
        functools.partial(quarter_kernel, n),
        out_shape=[jax.ShapeDtypeStruct(a.shape, a.dtype) for a in arrays],
        in_specs=vmem_specs(n),
        out_specs=vmem_specs(n),
        scratch_shapes=[pltpu.SemaphoreType.DMA((3, n)), pltpu.SemaphoreType.DMA((3, n))],
        compiler_params=params(collective_id),
        name="swap_quarters",
    )(*arrays)


CHUNKS = 4


def rows_kernel(x, o, send, recv, send_on, recv_on, sems):
    d, c, m = lax.axis_index("dp"), lax.axis_index("c"), lax.axis_index("mp")
    me, far = 2 * d + c, 2 * (1 - d) + c
    core = {"c": 1 - c}
    across = {"dp": 1 - d, "mp": 1 - m}
    greet([core, across])
    step = ROWS // CHUNKS
    first = []
    for k in range(CHUNKS):
        rows = pl.ds(k * step, step)
        copy = remote(x.at[rows], o.at[me, rows], send.at[k], recv.at[k], across)
        copy.start()
        first.append(copy)
    near = remote(x, o.at[me], sems.at[0], sems.at[1], core)
    near.start()
    o[me] = x[...]
    onward = []
    for k in range(CHUNKS):
        rows = pl.ds(k * step, step)
        first[k].wait_recv()
        copy = remote(o.at[far, rows], o.at[far, rows], send_on.at[k], recv_on.at[k], core)
        copy.start()
        onward.append(copy)
    near.wait()
    for k in range(CHUNKS):
        onward[k].wait()
        first[k].wait_send()


def gather_rows(x):
    dma = pltpu.SemaphoreType.DMA
    out = pl.pallas_call(
        rows_kernel,
        out_shape=jax.ShapeDtypeStruct((4, *x.shape), x.dtype),
        in_specs=vmem_specs(1),
        out_specs=vmem_specs(1)[0],
        scratch_shapes=[dma((CHUNKS,)), dma((CHUNKS,)), dma((CHUNKS,)), dma((CHUNKS,)), dma((2,))],
        compiler_params=params(1),
        name="gather_rows",
    )(x)
    return out.reshape(4 * x.shape[0], x.shape[1])


def sum_kernel(x, o, from_core, s_here, s_send, from_across, t_send, from_copy, *sems):
    send0, recv0, send1, recv1, send2, recv2 = sems
    d, c, m = lax.axis_index("dp"), lax.axis_index("c"), lax.axis_index("mp")
    core = {"c": 1 - c}
    across = {"dp": 1 - d, "mp": 1 - m}
    copy_of = {"mp": 1 - m}
    greet([core, across, copy_of])
    step = ROWS // CHUNKS
    rows = [pl.ds(k * step, step) for k in range(CHUNKS)]
    zero, one, two = [], [], []
    for k in range(CHUNKS):
        copy = remote(x.at[:, 1 - c, rows[k]], from_core.at[:, rows[k]], send0.at[k], recv0.at[k], core)
        copy.start()
        zero.append(copy)
    for k in range(CHUNKS):
        zero[k].wait_recv()
        s_send[rows[k]] = (
            x[1 - d, c, rows[k]].astype(f32) + from_core[1 - d, rows[k]].astype(f32)
        ).astype(bf16)
        copy = remote(s_send.at[rows[k]], from_across.at[rows[k]], send1.at[k], recv1.at[k], across)
        copy.start()
        one.append(copy)
        s_here[rows[k]] = x[d, c, rows[k]].astype(f32) + from_core[d, rows[k]].astype(f32)
    for k in range(CHUNKS):
        one[k].wait_recv()
        t_send[rows[k]] = (s_here[rows[k]] + from_across[rows[k]].astype(f32)).astype(bf16)
        copy = remote(t_send.at[rows[k]], from_copy.at[rows[k]], send2.at[k], recv2.at[k], copy_of)
        copy.start()
        two.append(copy)
    for k in range(CHUNKS):
        two[k].wait_recv()
        o[rows[k]] = t_send[rows[k]].astype(f32) + from_copy[rows[k]].astype(f32)
    for k in range(CHUNKS):
        zero[k].wait_send()
        one[k].wait_send()
        two[k].wait_send()


def sum_rows(x):
    wide = x.shape[-1]
    dma = pltpu.SemaphoreType.DMA
    return pl.pallas_call(
        sum_kernel,
        out_shape=jax.ShapeDtypeStruct((ROWS, wide), f32),
        in_specs=vmem_specs(1),
        out_specs=vmem_specs(1)[0],
        scratch_shapes=[
            pltpu.VMEM((2, ROWS, wide), bf16),
            pltpu.VMEM((ROWS, wide), f32),
            pltpu.VMEM((ROWS, wide), bf16),
            pltpu.VMEM((ROWS, wide), bf16),
            pltpu.VMEM((ROWS, wide), bf16),
            pltpu.VMEM((ROWS, wide), bf16),
        ]
        + [dma((CHUNKS,))] * 6,
        compiler_params=params(2),
        name="sum_rows",
    )(x.reshape(2, 2, ROWS, wide))


def ring(axis, size):
    me = lax.axis_index(axis)
    places = [lax.rem(me + k, size) for k in (1, 3, 2)]
    return me, places, [{axis: p} for p in places]


def spread_kernel(x, q, kv, *sems):
    sq, rq, sk, rk, sy, ry = sems
    z, zs, z_peers = ring("z", 4)
    y, ys, y_peers = ring("y", 4)
    greet(z_peers + y_peers)
    first, last, along = [], [], []
    for k in range(3):
        copy = remote(x.at[zs[k], pl.ds(1, 2)], kv.at[z, y], sk.at[k], rk.at[k], z_peers[k])
        copy.start()
        first.append(copy)
    for k in range(3):
        copy = remote(x.at[zs[k], 0], q.at[z], sq.at[k], rq.at[k], z_peers[k])
        copy.start()
        last.append(copy)

    def onward(place, k):
        for j in range(3):
            copy = remote(kv.at[place, y], kv.at[place, y], sy.at[k, j], ry.at[k, j], y_peers[j])
            copy.start()
            along.append(copy)

    q[z] = x[z, 0]
    kv[z, y] = x[z, pl.ds(1, 2)]
    onward(z, 3)
    for k in range(3):
        first[k].wait_recv()
        onward(lax.rem(z + (3, 1, 2)[k], 4), k)
    for copy in last + along:
        copy.wait()
    for copy in first:
        copy.wait_send()


def spread(x):
    dma = pltpu.SemaphoreType.DMA
    return pl.pallas_call(
        spread_kernel,
        out_shape=[
            jax.ShapeDtypeStruct((4, BLOCK, HD), bf16),
            jax.ShapeDtypeStruct((4, 4, 2, BLOCK, HD), bf16),
        ],
        in_specs=vmem_specs(1),
        out_specs=vmem_specs(2),
        scratch_shapes=[dma((3,))] * 4 + [dma((4, 3))] * 2,
        compiler_params=params(3),
        name="spread",
    )(x)


def turn_kernel(x, o, send, recv):
    z, zs, z_peers = ring("z", 4)
    greet(z_peers)
    out = []
    for k in range(3):
        copy = remote(x.at[zs[k]], o.at[z], send.at[k], recv.at[k], z_peers[k])
        copy.start()
        out.append(copy)
    o[z] = x[z]
    for copy in out:
        copy.wait()


def turn(x):
    dma = pltpu.SemaphoreType.DMA
    return pl.pallas_call(
        turn_kernel,
        out_shape=jax.ShapeDtypeStruct(x.shape, x.dtype),
        in_specs=vmem_specs(1),
        out_specs=vmem_specs(1)[0],
        scratch_shapes=[dma((3,))] * 2,
        compiler_params=params(4),
        name="turn",
    )(x)


def collect_kernel(dq, dkv, o, from_y, total, *sems):
    sq, rq, sk, rk, sy, ry = sems
    z, zs, z_peers = ring("z", 4)
    y, ys, y_peers = ring("y", 4)
    greet(z_peers + y_peers)
    along, last = [], []
    order = [zs[0], zs[1], zs[2], z]
    for k in range(4):
        for j in range(3):
            copy = remote(
                dkv.at[order[k], ys[j]], from_y.at[j, k], sy.at[k, j], ry.at[k, j], y_peers[j]
            )
            copy.start()
            along.append(copy)
    for k in range(3):
        copy = remote(dq.at[zs[k]], o.at[z, 0], sq.at[k], rq.at[k], z_peers[k])
        copy.start()
        last.append(copy)
    o[z, 0] = dq[z]
    for k in range(4):
        for j in range(3):
            along[3 * k + j].wait_recv()
        summed = (
            dkv[order[k], y].astype(f32)
            + from_y[0, k].astype(f32)
            + from_y[1, k].astype(f32)
            + from_y[2, k].astype(f32)
        ).astype(bf16)
        if k < 3:
            total[k] = summed
            copy = remote(total.at[k], o.at[z, pl.ds(1, 2)], sk.at[k], rk.at[k], z_peers[k])
            copy.start()
            last.append(copy)
        else:
            o[z, pl.ds(1, 2)] = summed
    for copy in last:
        copy.wait()
    for copy in along:
        copy.wait_send()


def collect(dq, dkv):
    dma = pltpu.SemaphoreType.DMA
    return pl.pallas_call(
        collect_kernel,
        out_shape=jax.ShapeDtypeStruct((4, 3, BLOCK, HD), bf16),
        in_specs=vmem_specs(2),
        out_specs=vmem_specs(1)[0],
        scratch_shapes=[
            pltpu.VMEM((3, 4, 2, BLOCK, HD), bf16),
            pltpu.VMEM((3, 2, BLOCK, HD), bf16),
        ]
        + [dma((3,))] * 4
        + [dma((4, 3))] * 2,
        compiler_params=params(5),
        name="collect",
    )(dq, dkv)


def reach(info, block):
    t = block * BLOCK + lax.broadcasted_iota(jnp.int32, (BLOCK, 1), 0)
    begin = jnp.where(t >= info[2], info[2], jnp.where(t >= info[1], info[1], info[0]))
    end = jnp.minimum((t // FRAME + 1) * FRAME, info[3])
    living = t < info[3]
    return jnp.where(living, begin, t), jnp.where(living, end, t + 1)


def dot_t(a, b):
    return lax.dot_general(a, b, (((1,), (1,)), ((), ())), preferred_element_type=f32)


def dot_l(a, b):
    return lax.dot_general(a, b, (((0,), (0,)), ((), ())), preferred_element_type=f32)


def visible_scores(q, k, j, low, high):
    s = dot_t(q, k) * scale
    at = j * BLOCK + lax.broadcasted_iota(jnp.int32, (1, BLOCK), 1)
    return jnp.where((at >= low) & (at < high), s, -1e30)


def attend_kernel(info, q_ref, kv_ref, o_ref, lse_ref):
    block = 4 * pl.program_id(0) + info[4]
    low, high = reach(info, block)
    q = q_ref[0]

    def step(j, state):
        top, total, acc = state
        s = visible_scores(q, kv_ref[j, 0], j, low, high)
        now = jnp.maximum(top, jnp.max(s, -1, keepdims=True))
        p = jnp.exp(s - now)
        shrink = jnp.exp(top - now)
        total = total * shrink + jnp.sum(p, -1, keepdims=True)
        acc = acc * shrink + jnp.dot(p.astype(bf16), kv_ref[j, 1], preferred_element_type=f32)
        return now, total, acc

    top, total, acc = lax.fori_loop(
        0,
        block + 1,
        step,
        (jnp.full((BLOCK, 1), -1e30, f32), jnp.zeros((BLOCK, 1), f32), jnp.zeros((BLOCK, HD), f32)),
    )
    o_ref[0] = acc / total
    lse_ref[0] = jnp.broadcast_to(top + jnp.log(total), (BLOCK, HD))


def attend(info, q, kv):
    return pl.pallas_call(
        attend_kernel,
        grid=(4,),
        out_shape=[jax.ShapeDtypeStruct((4, BLOCK, HD), f32)] * 2,
        in_specs=[
            pl.BlockSpec(memory_space=pltpu.SMEM),
            pl.BlockSpec((1, BLOCK, HD), lambda i: (i, 0, 0)),
            pl.BlockSpec((16, 2, BLOCK, HD), lambda i: (0, 0, 0, 0)),
        ],
        out_specs=[pl.BlockSpec((1, BLOCK, HD), lambda i: (i, 0, 0))] * 2,
        compiler_params=params(),
        cost_estimate=pl.CostEstimate(flops=20 * 10**9, bytes_accessed=4 * 10**6, transcendentals=10**6),
        name="attend",
    )(info, q, kv.reshape(16, 2, BLOCK, HD))


def attend_back_kernel(info, q_ref, kv_ref, o_ref, lse_ref, do_ref, dq_ref, dkv_ref, acc):
    i = pl.program_id(0)
    block = 4 * i + info[4]
    low, high = reach(info, block)
    q, do = q_ref[0], do_ref[0]
    lse = lse_ref[0][:, :1]
    inner = jnp.sum(o_ref[0] * do.astype(f32), -1, keepdims=True)

    @pl.when(i == 0)
    def _():
        acc[...] = jnp.zeros_like(acc)

    def step(j, dq):
        k, v = kv_ref[j, 0], kv_ref[j, 1]
        p = jnp.exp(visible_scores(q, k, j, low, high) - lse)
        acc[j, 1] += dot_l(p.astype(bf16), do)
        ds = (p * (dot_t(do, v) - inner)).astype(bf16)
        acc[j, 0] += dot_l(ds, q)
        return dq + jnp.dot(ds, k, preferred_element_type=f32)

    dq = lax.fori_loop(0, block + 1, step, jnp.zeros((BLOCK, HD), f32))
    dq_ref[0] = (dq * scale).astype(bf16)

    @pl.when(i == 3)
    def _():
        def cast(j, _):
            dkv_ref[j, 0] = (acc[j, 0] * scale).astype(bf16)
            dkv_ref[j, 1] = acc[j, 1].astype(bf16)
            return 0

        lax.fori_loop(0, 16, cast, 0)


def attend_back(info, q, kv, o, lse, do):
    dq, dkv = pl.pallas_call(
        attend_back_kernel,
        grid=(4,),
        out_shape=[
            jax.ShapeDtypeStruct((4, BLOCK, HD), bf16),
            jax.ShapeDtypeStruct((16, 2, BLOCK, HD), bf16),
        ],
        in_specs=[
            pl.BlockSpec(memory_space=pltpu.SMEM),
            pl.BlockSpec((1, BLOCK, HD), lambda i: (i, 0, 0)),
            pl.BlockSpec((16, 2, BLOCK, HD), lambda i: (0, 0, 0, 0)),
        ]
        + [pl.BlockSpec((1, BLOCK, HD), lambda i: (i, 0, 0))] * 3,
        out_specs=[
            pl.BlockSpec((1, BLOCK, HD), lambda i: (i, 0, 0)),
            pl.BlockSpec((16, 2, BLOCK, HD), lambda i: (0, 0, 0, 0)),
        ],
        scratch_shapes=[pltpu.VMEM((16, 2, BLOCK, HD), f32)],
        compiler_params=params(),
        cost_estimate=pl.CostEstimate(flops=30 * 10**9, bytes_accessed=8 * 10**6, transcendentals=10**6),
        name="attend_back",
    )(info, q, kv.reshape(16, 2, BLOCK, HD), o, lse, do)
    return dq, dkv.reshape(4, 4, 2, BLOCK, HD)


def to_inner(x):
    return x.reshape(-1, 2, 16, 64).swapaxes(1, 2).reshape(-1, D)


def to_outer(x):
    return x.reshape(-1, 16, 2, 64).swapaxes(1, 2).reshape(-1, D)


def norm(value):
    centre = value - jnp.mean(value, -1, keepdims=True)
    r = lax.rsqrt(jnp.mean(centre * centre, -1, keepdims=True) + epsilon)
    return centre * r, r


def norm_back(grad, n, r, gain):
    e = grad * gain
    return r * (e - jnp.mean(e, -1, keepdims=True) - n * jnp.mean(e * n, -1, keepdims=True))


def turned(x, cosine, sine, direction):
    a, b = x[..., :64], x[..., 64:]
    return jnp.concatenate([a * cosine - direction * b * sine, direction * a * sine + b * cosine], -1)


def quarters(w):
    return w.reshape(w.shape[0], 4, -1).swapaxes(0, 1)


def joined(w):
    return w.swapaxes(0, 1).reshape(w.shape[1], -1)


def gelu(v):
    return jax.nn.gelu(v, approximate=False)


def gather_weights(x):
    return lax.all_gather(x, ZY, axis=0, tiled=True)


def scatter_grads(x):
    return lax.psum_scatter(x, ZY, scatter_dimension=0, tiled=True)


def local(
    inputs,
    clip_starts,
    pad_lengths,
    w_query,
    w_key,
    w_value,
    w_out,
    w_up,
    w_down,
    gain_first,
    gain_second,
    cotangent,
):
    z, y = lax.axis_index("z"), lax.axis_index("y")
    living = LEN - pad_lengths
    side = jnp.concatenate(
        [
            gain_first[:, None],
            gain_second[:, None],
            jnp.broadcast_to(clip_starts, (32, 3)).astype(bf16),
            jnp.broadcast_to(pad_lengths[None], (32, 1)).astype(bf16),
            jnp.zeros((32, HD - 6), bf16),
        ],
        1,
    )
    first = jnp.concatenate(
        [quarters(w_query), quarters(w_key), quarters(w_value), jnp.broadcast_to(side, (4, 32, HD))], -1
    )
    second = jnp.concatenate([quarters(w_out.T), quarters(w_up)], -1)
    third = quarters(w_down.T)
    first, second, third = swap_quarters(0, first, second, third)
    first = gather_weights(first.reshape(HD, -1))
    second = gather_weights(second.reshape(HD, -1))
    down = gather_weights(third.reshape(HD, -1))

    side = first[:, 768:]
    gains = side[:, :2].astype(f32).T
    gain_one, gain_two = gains[0], gains[1]
    facts = side[:128:64, 2:6].astype(jnp.int32)
    begins, ends = facts[:, :3], LEN - facts[:, 3]

    x = to_inner(inputs[0]).astype(f32)
    n_one, r_one = norm(x)
    normed_one = gather_rows((n_one * gain_one).astype(bf16))
    incoming = to_inner(cotangent[0])
    incoming_all = gather_rows(incoming)

    places = (4 * z + y) * BLOCK + jnp.arange(BLOCK, dtype=jnp.int32)
    opened = begins[:, None, :] <= places[None, :, None]
    position = places - jnp.max(jnp.where(opened, begins[:, None, :], 0), -1)
    frequency = 10000.0 ** (-2.0 * jnp.arange(HD // 2, dtype=f32) / HD)
    angles = position.astype(f32)[..., None] * frequency
    cosine, sine = jnp.cos(angles)[:, :, None], jnp.sin(angles)[:, :, None]

    lin = jnp.dot(normed_one, first, preferred_element_type=f32)
    lin = lin[:, :768].reshape(2, BLOCK, 3, 2, HD)
    query = turned(lin[:, :, 0], cosine, sine, 1.0)
    key = turned(lin[:, :, 1], cosine, sine, 1.0)
    qkv = jnp.stack([query, key, lin[:, :, 2]], 0).astype(bf16)
    qkv = qkv.transpose(1, 3, 0, 2, 4).reshape(4, 3, BLOCK, HD)
    q, kv = spread(qkv)
    mine = z // 2
    info = jnp.concatenate(
        [lax.dynamic_index_in_dim(begins, mine, 0, False), lax.dynamic_index_in_dim(ends, mine, 0), y[None]]
    ).astype(jnp.int32)
    o, lse = attend(info, q, kv)
    mixed = turn(o.astype(bf16))
    mixed = mixed.reshape(2, 2, BLOCK, HD).swapaxes(1, 2).reshape(512, 2 * HD)

    out = second[:, :256]
    middle = x + sum_rows(dot_t(mixed, out).astype(bf16))
    n_two, r_two = norm(middle)
    normed_two = gather_rows((n_two * gain_two).astype(bf16))
    hidden = jnp.dot(normed_two, second, preferred_element_type=f32)[:, 256:]
    active, pull = jax.vjp(gelu, hidden)
    active = active.astype(bf16)
    grad_active = jnp.dot(incoming_all, down, preferred_element_type=f32)
    grad_hidden = pull(grad_active)[0].astype(bf16)
    grad_normed_two = sum_rows(dot_t(jnp.pad(grad_hidden, ((0, 0), (256, 0))), second).astype(bf16))
    grad_middle = incoming.astype(f32) + norm_back(grad_normed_two, n_two, r_two, gain_two)
    branch = gather_rows(grad_middle.astype(bf16))

    grad_down = scatter_grads(dot_l(incoming_all, active).astype(bf16))
    grad_up = scatter_grads(dot_l(normed_two, grad_hidden).astype(bf16))

    grad_mixed = jnp.dot(branch, out, preferred_element_type=f32).astype(bf16)
    grad_mixed = grad_mixed.reshape(2, BLOCK, 2, HD).swapaxes(1, 2).reshape(4, BLOCK, HD)
    grad_out = scatter_grads(dot_l(branch, mixed).astype(bf16))
    dq, dkv = attend_back(info, q, kv, o, lse, turn(grad_mixed))
    output = middle + sum_rows(dot_t(active, down).astype(bf16))
    grads = collect(dq, dkv).reshape(2, 2, 3, BLOCK, HD).transpose(2, 0, 3, 1, 4)
    grad_query = turned(grads[0].astype(f32), cosine, sine, -1.0).astype(bf16)
    grad_key = turned(grads[1].astype(f32), cosine, sine, -1.0).astype(bf16)
    grad_lin = jnp.stack([grad_query, grad_key, grads[2]], 2).reshape(512, 768)

    grad_normed_one = sum_rows(dot_t(jnp.pad(grad_lin, ((0, 0), (0, HD))), first).astype(bf16))
    grad_input = grad_middle + norm_back(grad_normed_one, n_one, r_one, gain_one)
    gain_grads = jnp.stack([jnp.sum(grad_normed_one * n_one, 0), jnp.sum(grad_normed_two * n_two, 0)], 1)
    grad_first = jnp.concatenate(
        [dot_l(normed_one, grad_lin).astype(bf16), jnp.pad(gain_grads, ((0, 0), (0, HD - 2))).astype(bf16)], 1
    )
    grad_first = scatter_grads(grad_first)

    grad_first, grad_out, grad_up, grad_down = swap_quarters(
        6, *[g.reshape(4, 32, -1) for g in (grad_first, grad_out, grad_up, grad_down)]
    )
    grad_first, grad_out, grad_up, grad_down = [
        g.astype(f32) for g in (grad_first, grad_out, grad_up, grad_down)
    ]
    gain_grads = jnp.sum(grad_first[:, :, 768:770], 0)
    return (
        to_outer(output).astype(bf16)[None],
        to_outer(grad_input)[None],
        joined(grad_first[:, :, :256]),
        joined(grad_first[:, :, 256:512]),
        joined(grad_first[:, :, 512:768]),
        joined(grad_out).T,
        joined(grad_up),
        joined(grad_down).T,
        gain_grads[:, 0],
        gain_grads[:, 1],
    )


def solution(mesh):
    split = Mesh(mesh.devices.reshape(2, 4, 4, 2, 2), ("dp", "z", "y", "c", "mp"))
    seq = ("z", "y", "c")
    weights = ("dp", "z", "y", "c")
    tokens = P("dp", seq, None)
    wide, tall = P(weights, "mp"), P("mp", weights)
    return jax.shard_map(
        local,
        mesh=split,
        in_specs=(tokens, P("dp", None), P("dp"), wide, wide, wide, tall, wide, tall, P(weights), P(weights), tokens),
        out_specs=(tokens, tokens, wide, wide, wide, tall, wide, tall, P(weights), P(weights)),
        check_vma=False,
    )
```

time: 1810 us -> 746 us (0.41); the launches traced: 1780 us -> 741 us
  waiting for transfers between devices: 884 us -> 278 us
  blocking collectives: 441 us -> 0 us
  Pallas kernels: 0 us -> 317 us
  matrix products: 206 us -> 49.3 us
  local copies, waits for them, and re-layouts: 181 us -> 58 us
    unnamed x2 -> x0, blocking collectives: 357 us -> none
    reduce_scatter x5 -> x4, waiting for transfers between devices: 577 us -> 241 us  [scatter_grads(): return lax.psum_scatter(x, ZY, scatter_dimension=0, tiled=True)]
    pallas_call x0 -> x16, Pallas kernels: none -> 317 us  [the longest x4 86.8 us: sum_rows(): pl.pallas_call(sum_kernel, out_shape=jax.ShapeDtypeStruct((ROWS, wide), f...]
    all_gather x3, waiting for transfers between devices: 293 us -> 35.3 us  [gather_weights(): return lax.all_gather(x, ZY, axis=0, tiled=True)]
    dot_general x26 -> x12, matrix products: 206 us -> 49.3 us  [the longest x4 14.8 us: dot_l(): lax.dot_general(a, b, (((0,), (0,)), ((), ())), preferred_element_type=f32)]
    transpose x2 -> x6, local copies, waits for them, and re-layouts: 62.8 us -> 2.64 us  [the longest x1 0.88 us: quarters(): return w.reshape(w.shape[0], 4, -1).swapaxes(0, 1)]
    all_to_all x2 -> x0, blocking collectives: 55.6 us -> none  [from_everyone(): return lax.all_to_all(copies, axis, split_axis=0, concat_axis=0, tiled=True)]
    dot_general x6 -> x0, local copies, waits for them, and re-layouts: 29.1 us -> none  [the longest x4 28.5 us: project(): jnp.dot(normed_one, weight, preferred_element_type=jnp.float32)]
  transfers between devices with their start and end apart: 12 -> 7, of which waited for: 6 -> 5; matrix products, arithmetic and copies ran while one was open for 17% -> 11% of each run, Pallas kernels for 0% -> 22%
where the time goes in v1:
time: 746 us; the launch traced here: 741 us
  Pallas kernels  317 us (42%)
  waiting for transfers between devices  278 us (37%)
  local copies, waits for them, and re-layouts  58 us (8%)
  matrix products  49.3 us (7%)
  other arithmetic  22.6 us (3%)
  between operations  15.9 us (2%)
    reduce_scatter x4, waiting for transfers between devices, scatter_grads(): return lax.psum_scatter(x, ZY, scatter_dimension=0, tiled=True)  241 us
    pallas_call x4, Pallas kernels, sum_rows(): pl.pallas_call(sum_kernel, out_shape=jax.ShapeDtypeStruct((ROWS, wide), f...  86.8 us
    pallas_call x4, Pallas kernels, gather_rows(): pl.pallas_call(rows_kernel, out_shape=jax.ShapeDtypeStruct((4, *x.shape),...  67.8 us
    pallas_call x1, Pallas kernels, spread(): pl.pallas_call(spread_kernel, out_shape=[jax.ShapeDtypeStruct((4, BLOCK,...  42.6 us
    pallas_call x1, Pallas kernels, collect(): pl.pallas_call(collect_kernel, out_shape=jax.ShapeDtypeStruct((4, 3, BLOC...  37.5 us
    all_gather x3, waiting for transfers between devices, gather_weights(): return lax.all_gather(x, ZY, axis=0, tiled=True)  35.3 us
    pallas_call x2, Pallas kernels, swap_quarters(): pl.pallas_call(functools.partial(quarter_kernel, n), out_shape=[jax.Shape...  30.3 us
    unnamed x77, local copies, waits for them, and re-layouts  30.2 us
  transfers between devices with their start and end apart: 7, of which 5 were waited for; matrix products, arithmetic and copies ran while one was open for 11% of the time, Pallas kernels for 22%

profile of v1, /device:TPU:1, one launch (start us, length us, event | category | flops | bytes accessed | tf_op | source)
XLA Modules:
  0.0 741.2 jit_solution(3128881976513759605)
XLA Ops:
  14.8 15.1 %swap_quarters.2 = (bf16[4,32,896]{2,1,0:T(8,128)(2,1)S(1)}, bf16[4,32,1280]{2,1,0:T(8,128)(2,1)}, bf16[4,32,1024]{2,1,0:T(8,128)(2,1)}) custom-call(bf16[4,32,896]{2,1,0:T(8,128)(2,1)S(1)} %pad_maximum_fusion.3.refs_0_, bf16[4,32,1280]{2,1,0:T(8,128)(2,1)S(1)} %pad_maximum_fusion.2.refs_1_, bf16[4,32,1024]{2,1,0:T(8,128)(2,1)S(1)} %bitcast.222), custom_call_target="tpu_custom_call" | custom-call | tf_op jit(solution)/shard_map/swap_quarters/pallas_call | solution.py:70
  35.4 16.6 %gather_rows.6 = bf16[4,128,2048]{2,1,0:T(8,128)(2,1)S(1)} custom-call(bf16[128,2048]{1,0:T(8,128)(2,1)S(1)} %copy.228.x), custom_call_target="tpu_custom_call" | custom-call | tf_op jit(solution)/shard_map/gather_rows/pallas_call | solution.py:115
  52.1 35.3 %all-gather.4.cloned.1.call-done = bf16[2048,896]{0,1:T(8,128)(2,1)} async-done(((bf16[128,896]{0,1:T(8,128)(2,1)}), bf16[2048,896]{0,1:T(8,128)(2,1)}) %all-gather.4.cloned.1.call-update) | async-done | bytes 3670032 | tf_op jit(solution)/shard_map/all_gather | solution.py:487
  91.7 17.9 %gather_rows.4 = bf16[4,128,2048]{2,1,0:T(8,128)(2,1)S(1)} custom-call(bf16[128,2048]{1,0:T(8,128)(2,1)S(1)} %multiply_convert_fusion.2.x), custom_call_target="tpu_custom_call" | custom-call | tf_op jit(solution)/shard_map/gather_rows/pallas_call | solution.py:115
  125.9 42.6 %spread.1 = (bf16[4,256,128]{2,1,0:T(8,128)(2,1)S(1)}, bf16[4,4,2,256,128]{4,3,2,1,0:T(8,128)(2,1)S(1)}) custom-call(bf16[4,3,256,128]{3,2,1,0:T(8,128)(2,1)S(1)} %bitcast.208), custom_call_target="tpu_custom_call" | custom-call | tf_op jit(solution)/shard_map/spread/pallas_call | solution.py:228
  169.3 14.1 %attend.1 = (f32[4,256,128]{2,1,0:T(8,128)S(1)}, f32[4,256,128]{2,1,0:T(8,128)S(1)}) custom-call(s32[5]{0:T(128)S(1)} %pad_add_fusion.info, bf16[4,256,128]{2,1,0:T(8,128)(2,1)S(1)} %get-tuple-element.24.q_ref, bf16[16,2,256,128]{3,2,1,0:T(8,128)(2,1)S(1)} %bitcast.230), custom_call_target="tpu_custom_call" | custom-call | flops 20000000000 | bytes 4000000 | tf_op jit(solution)/shard_map/attend/pallas_call | solution.py:375
  184.3 8.3 %turn.2 = bf16[4,256,128]{2,1,0:T(8,128)(2,1)S(1)} custom-call(bf16[4,256,128]{2,1,0:T(8,128)(2,1)S(1)} %convert_element_type.169.x), custom_call_target="tpu_custom_call" | custom-call | tf_op jit(solution)/shard_map/turn/pallas_call | solution.py:257
  195.7 22.2 %sum_rows.4 = f32[128,2048]{1,0:T(8,128)S(1)} custom-call(bf16[2,2,128,2048]{3,2,1,0:T(8,128)(2,1)S(1)} %bitcast.207), custom_call_target="tpu_custom_call" | custom-call | tf_op jit(solution)/shard_map/sum_rows/pallas_call | solution.py:168
  218.6 16.7 %gather_rows.5 = bf16[4,128,2048]{2,1,0:T(8,128)(2,1)S(1)} custom-call(bf16[128,2048]{1,0:T(8,128)(2,1)S(1)} %multiply_convert_fusion.1.x), custom_call_target="tpu_custom_call" | custom-call | tf_op jit(solution)/shard_map/gather_rows/pallas_call | solution.py:115
  236.6 8.2 %multiply_convert_fusion = (bf16[512,1024]{1,0:T(8,128)(2,1)}, f32[512,1024]{1,0:T(8,128)}, f32[512,1024]{1,0:T(8,128)}) fusion(bf16[512,2048]{1,0:T(8,128)(2,1)S(1)} %bitcast.214, bf16[2048,1280]{1,0:T(8,128)(2,1)S(1)} %bitcast.254), kind=kOutput, calls=%fused_computation.24 | convolution fusion | flops 2181562368 | bytes 11534336 | tf_op jit(solution)/shard_map/dot_general | solution.py:568
  249.9 19.3 %sum_rows.5 = f32[128,2048]{1,0:T(8,128)S(1)} custom-call(bf16[2,2,128,2048]{3,2,1,0:T(8,128)(2,1)S(1)} %bitcast.220), custom_call_target="tpu_custom_call" | custom-call | tf_op jit(solution)/shard_map/sum_rows/pallas_call | solution.py:168
  278.5 22.5 %sum_rows.6 = f32[128,2048]{1,0:T(8,128)S(1)} custom-call(bf16[2,2,128,2048]{3,2,1,0:T(8,128)(2,1)S(1)} %bitcast.221), custom_call_target="tpu_custom_call" | custom-call | tf_op jit(solution)/shard_map/sum_rows/pallas_call | solution.py:168
  303.1 16.5 %gather_rows.7 = bf16[4,128,2048]{2,1,0:T(8,128)(2,1)S(1)} custom-call(bf16[128,2048]{1,0:T(8,128)(2,1)S(1)} %get-tuple-element.94.x), custom_call_target="tpu_custom_call" | custom-call | tf_op jit(solution)/shard_map/gather_rows/pallas_call | solution.py:115
  328.8 6.6 turn.3.do_ref
  337.0 23.3 %attend_back.1 = (bf16[4,256,128]{2,1,0:T(8,128)(2,1)S(1)}, bf16[16,2,256,128]{3,2,1,0:T(8,128)(2,1)S(1)}) custom-call(s32[5]{0:T(128)S(1)} %pad_add_fusion.info, bf16[4,256,128]{2,1,0:T(8,128)(2,1)S(1)} %get-tuple-element.24.q_ref, bf16[16,2,256,128]{3,2,1,0:T(8,128)(2,1)S(1)} %bitcast.231, f32[4,256,128]{2,1,0:T(8,128)S(1)} %get-tuple-element.26.o_ref, ...), custom_call_target="tpu_custom_call" | custom-call | flops 30000001024 | bytes 8000000 | tf_op jit(solution)/shard_map/attend_back/pallas_call | solution.py:425
  360.3 37.5 %collect.1 = bf16[4,3,256,128]{3,2,1,0:T(8,128)(2,1)S(1)} custom-call(bf16[4,256,128]{2,1,0:T(8,128)(2,1)S(1)} %get-tuple-element.30.dq, bf16[4,4,2,256,128]{4,3,2,1,0:T(8,128)(2,1)S(1)} %bitcast.218), custom_call_target="tpu_custom_call" | custom-call | tf_op jit(solution)/shard_map/collect/pallas_call | solution.py:311
  409.5 22.9 %sum_rows.7 = f32[128,2048]{1,0:T(8,128)S(1)} custom-call(bf16[2,2,128,2048]{3,2,1,0:T(8,128)(2,1)S(1)} %bitcast.219), custom_call_target="tpu_custom_call" | custom-call | tf_op jit(solution)/shard_map/sum_rows/pallas_call | solution.py:168
  437.9 6.1 copy.248
  444.2 5.6 convert_bitcast_fusion
  449.8 6.4 copy.250
  469.8 79.4 %reduce-scatter.13.cloned.1.call-done = bf16[128,896]{1,0:T(8,128)(2,1)} async-done(((bf16[2048,896]{1,0:T(8,128)(2,1)}), bf16[128,896]{1,0:T(8,128)(2,1)}) %reduce-scatter.13.cloned.1.call-update) | async-done | bytes 229392 | tf_op jit(solution)/shard_map/reduce_scatter | solution.py:491
  549.1 80.6 %reduce-scatter.15.cloned.1.call-done = bf16[128,1024]{1,0:T(8,128)(2,1)} async-done(((bf16[2048,1024]{1,0:T(8,128)(2,1)}), bf16[128,1024]{1,0:T(8,128)(2,1)}) %reduce-scatter.15.cloned.1.call-update) | async-done | bytes 262160 | tf_op jit(solution)/shard_map/reduce_scatter | solution.py:491
  629.7 80.3 %reduce-scatter.11.cloned.1.call-done = bf16[128,1024]{1,0:T(8,128)(2,1)} async-done(((bf16[2048,1024]{1,0:T(8,128)(2,1)}), bf16[128,1024]{1,0:T(8,128)(2,1)}) %reduce-scatter.11.cloned.1.call-update) | async-done | bytes 262160 | tf_op jit(solution)/shard_map/reduce_scatter | solution.py:491
  713.8 15.2 %swap_quarters.3 = (bf16[4,32,896]{2,1,0:T(8,128)(2,1)S(1)}, bf16[4,32,256]{2,1,0:T(8,128)(2,1)S(1)}, bf16[4,32,1024]{2,1,0:T(8,128)(2,1)S(1)}, bf16[4,32,1024]{2,1,0:T(8,128)(2,1)S(1)}) custom-call(bf16[4,32,896]{2,1,0:T(8,128)(2,1)S(1)} %bitcast.228, bf16[4,32,256]{2,1,0:T(8,128)(2,1)S(1)} %bitcast.229, bf16[4,32,1024]{2,1,0:T(8,128)(2,1)S(1)} %bitcast.226, ...), custom_call_target="tpu_custom_call" | custom-call | tf_op jit(solution)/shard_map/swap_quarters/pallas_call | solution.py:70
  (196 shorter events, 106.1 us)
Async XLA Ops:
  7.2 80.2 %all-gather.4.cloned.1.call-start = ((), (), s32[]{:S(2)}) async-start(), calls=%async_computation.4 | async-start | bytes 3899392 | tf_op jit(solution)/shard_map/all_gather | solution.py:487
  12.7 19.7 %copy-start.24 = (bf16[1,128,2048]{2,1,0:T(8,128)(2,1)S(1)}, bf16[1,128,2048]{2,1,0:T(8,128)(2,1)}, u32[]{:S(2)}) copy-start(bf16[1,128,2048]{2,1,0:T(8,128)(2,1)} %param.12) | copy-start | bytes 1572868
  30.8 162.8 %all-gather.6.cloned.1.call-start = ((), (), s32[]{:S(2)}) async-start(), calls=%async_computation.5 | async-start | bytes 5570560 | tf_op jit(solution)/shard_map/all_gather | solution.py:487
  31.6 213.2 %all-gather.8.cloned.1.call-start = ((), (), s32[]{:S(2)}) async-start(), calls=%async_computation.6 | async-start | bytes 4456448 | tf_op jit(solution)/shard_map/all_gather | solution.py:487
  32.3 437.4 %reduce-scatter.9.cloned.1.call-start = ((), (), s32[]{:S(2)}) async-start(), calls=%async_computation.7 | async-start | bytes 1114112 | tf_op jit(solution)/shard_map/reduce_scatter | solution.py:491
  90.1 20.8 %copy-start.26 = (bf16[2048,896]{0,1:T(8,128)(2,1)S(1)}, bf16[2048,896]{0,1:T(8,128)(2,1)}, u32[]{:S(2)}) copy-start(bf16[2048,896]{0,1:T(8,128)(2,1)} %all-gather.4.cloned.1.call-done) | copy-start | bytes 11010052
  168.6 14.9 %copy-start.9 = (bf16[4,4,2,256,128]{4,3,2,1,0:T(8,128)(2,1)}, bf16[4,4,2,256,128]{4,3,2,1,0:T(8,128)(2,1)S(1)}, u32[]{:S(2)}) copy-start(bf16[4,4,2,256,128]{4,3,2,1,0:T(8,128)(2,1)S(1)} %get-tuple-element.25) | copy-start | bytes 6291460
  195.7 22.2 %copy-start.15 = (f32[128,2048]{1,0:T(8,128)S(1)}, f32[128,2048]{1,0:T(8,128)}, u32[]{:S(2)}) copy-start(f32[128,2048]{1,0:T(8,128)} %copy.223) | copy-start | bytes 3145732
  195.7 40.9 %slice-start = ((s8[5242880]{0:T(1024)(128)(4,1)}), s8[4194304]{0:T(1024)(128)(4,1)S(1)}, s32[]{:S(2)}) async-start(s8[5242880]{0:T(1024)(128)(4,1)} %bitcast.253), calls=%async_computation.11 | async-start | bytes 8388608
  217.9 18.7 %slice-start.1 = ((s8[5242880]{0:T(1024)(128)(4,1)}), s8[1048576]{0:T(1024)(128)(4,1)S(1)}, s32[]{:S(2)}) async-start(s8[5242880]{0:T(1024)(128)(4,1)} %bitcast.253), calls=%async_computation.12 | async-start | bytes 2097152
  218.1 17.2 %copy-start.13 = (f32[128,2048]{1,0:T(8,128)}, f32[128,2048]{1,0:T(8,128)S(1)}, u32[]{:S(2)}) copy-start(f32[128,2048]{1,0:T(8,128)S(1)} %get-tuple-element.99) | copy-start | bytes 3145732
  244.8 24.4 %copy-start.28 = (f32[512,1024]{1,0:T(8,128)S(1)}, f32[512,1024]{1,0:T(8,128)}, u32[]{:S(2)}) copy-start(f32[512,1024]{1,0:T(8,128)} %get-tuple-element.126) | copy-start | bytes 6291460
  249.9 19.3 %copy-start.27 = (f32[512,1024]{1,0:T(8,128)S(1)}, f32[512,1024]{1,0:T(8,128)}, u32[]{:S(2)}) copy-start(f32[512,1024]{1,0:T(8,128)} %get-tuple-element.97) | copy-start | bytes 6291460
  249.9 25.4 %slice-start.2 = ((s8[5242880]{0:T(1024)(128)(4,1)}), s8[4194304]{0:T(1024)(128)(4,1)S(1)}, s32[]{:S(2)}) async-start(s8[5242880]{0:T(1024)(128)(4,1)} %bitcast.255), calls=%async_computation.13 | async-start | bytes 8388608
  269.2 6.1 slice-start.3
  278.5 22.5 %copy-start.14 = (f32[128,2048]{1,0:T(8,128)S(1)}, f32[128,2048]{1,0:T(8,128)}, u32[]{:S(2)}) copy-start(f32[128,2048]{1,0:T(8,128)} %copy-done.13) | copy-start | bytes 3145732
  303.1 17.9 %copy-start.22 = (bf16[2,2,256,128]{3,1,2,0:T(2,128)(2,1)S(1)}, bf16[2,2,256,128]{3,1,2,0:T(2,128)(2,1)}, u32[]{:S(2)}) copy-start(bf16[2,2,256,128]{3,1,2,0:T(2,128)(2,1)} %copy.222) | copy-start | bytes 786436
  322.8 12.6 %copy-start.12 = (f32[4,256,128]{2,1,0:T(8,128)S(1)}, f32[4,256,128]{2,1,0:T(8,128)}, u32[]{:S(2)}) copy-start(f32[4,256,128]{2,1,0:T(8,128)} %copy-done.11) | copy-start | bytes 1572868
  398.6 150.5 %reduce-scatter.13.cloned.1.call-start = ((), (), s32[]{:S(2)}) async-start(), calls=%async_computation.9 | async-start | bytes 3899392 | tf_op jit(solution)/shard_map/reduce_scatter | solution.py:491
  409.4 22.9 %copy-start.16 = (f32[128,2048]{1,0:T(8,128)S(1)}, f32[128,2048]{1,0:T(8,128)}, u32[]{:S(2)}) copy-start(f32[128,2048]{1,0:T(8,128)} %copy.223) | copy-start | bytes 3145732
  409.5 23.4 %copy-start.23 = (bf16[512,768]{1,0:T(8,128)(2,1)S(1)}, bf16[512,768]{1,0:T(8,128)(2,1)}, u32[]{:S(2)}) copy-start(bf16[512,768]{1,0:T(8,128)(2,1)} %reshape.339) | copy-start | bytes 2359300
  444.0 185.8 %reduce-scatter.15.cloned.1.call-start = ((), (), s32[]{:S(2)}) async-start(), calls=%async_computation.10 | async-start | bytes 4456448 | tf_op jit(solution)/shard_map/reduce_scatter | solution.py:491
  456.2 253.9 %reduce-scatter.11.cloned.1.call-start = ((), (), s32[]{:S(2)}) async-start(), calls=%async_computation.8 | async-start | bytes 4456448 | tf_op jit(solution)/shard_map/reduce_scatter | solution.py:491
  463.4 2.4 copy-start.17
  (17 other events, 21.6 us)
Sparse Core Ops, SparseCore 0:
  31.0 56.3 all-gather.3
  89.5 76.0 all-gather.5
  167.7 51.0 all-gather.7
  398.8 70.9 reduce-scatter.8
  473.3 75.7 reduce-scatter.12
  552.7 77.0 reduce-scatter.14
  633.1 76.9 reduce-scatter.10

commit v2 on v1

v2 whole, which is shorter than its diff:
```python
import functools

import jax
import jax.numpy as jnp
from jax import lax
from jax.experimental import pallas as pl
from jax.experimental.pallas import tpu as pltpu
from jax.sharding import Mesh
from jax.sharding import PartitionSpec as P

MESH = pl.DeviceIdType.MESH
HD = 128
FRAME = 32
LEN = 4096
D = 2048
ROWS = 128
BLOCK = 256
ZY = ("z", "y")
epsilon = 1e-05
scale = HD**-0.5
f32 = jnp.float32
bf16 = jnp.bfloat16


def params(collective_id=None, vmem=48, **kw):
    if collective_id is not None:
        kw = dict(collective_id=collective_id, has_side_effects=True, **kw)
    return pltpu.CompilerParams(vmem_limit_bytes=vmem * 2**20, **kw)


def vmem_specs(n):
    return [pl.BlockSpec(memory_space=pltpu.VMEM)] * n


def greet(peers):
    barrier = pltpu.get_barrier_semaphore()
    for peer in peers:
        pl.semaphore_signal(barrier, inc=1, device_id=peer, device_id_type=MESH)
    pl.semaphore_wait(barrier, len(peers))


def remote(src, dst, send, recv, peer):
    return pltpu.make_async_remote_copy(
        src_ref=src, dst_ref=dst, send_sem=send, recv_sem=recv, device_id=peer, device_id_type=MESH
    )


def started(copies, src, dst, send, recv, peer):
    copy = remote(src, dst, send, recv, peer)
    copy.start()
    copies.append(copy)
    return copy


class Sems:
    def __init__(self, send, recv):
        self.send, self.recv, self.used = send, recv, 0

    def take(self):
        k = self.used
        self.used += 1
        return self.send.at[k], self.recv.at[k]


def sem_pair(n):
    return [pltpu.SemaphoreType.DMA((n,)), pltpu.SemaphoreType.DMA((n,))]


def tensor_place():
    d, c, m = lax.axis_index("dp"), lax.axis_index("c"), lax.axis_index("mp")
    return d, c, m, {"c": 1 - c}, {"dp": 1 - d, "mp": 1 - m}, {"mp": 1 - m}


def ring(axis, size=4):
    me = lax.axis_index(axis)
    up, down, far = (lax.rem(me + k, size) for k in (1, size - 1, 2))
    return me, up, down, far, {axis: up}, {axis: down}


def added(*values):
    total = values[0].astype(f32)
    for v in values[1:]:
        total = total + v.astype(f32)
    return total


def run(*protocols):
    live = list(protocols)
    while live:
        for p in list(live):
            try:
                next(p)
            except StopIteration:
                live.remove(p)


def swap_plan(srcs, dsts, sems):
    d, c = lax.axis_index("dp"), lax.axis_index("c")
    me = 2 * d + c
    copies = []
    for a, b in [(d, 1 - c), (1 - d, c), (1 - d, 1 - c)]:
        for src, dst in zip(srcs, dsts):
            started(copies, src.at[2 * a + b], dst(me), *sems.take(), {"dp": a, "c": b})
    for src, dst in zip(srcs, dsts):
        dst(me)[...] = src[me]
    yield
    for copy in copies:
        copy.wait_recv()
    yield
    for copy in copies:
        copy.wait_send()


def swap_peers():
    d, c = lax.axis_index("dp"), lax.axis_index("c")
    return [{"dp": 1 - d}, {"dp": 1 - d, "c": 1 - c}]


def quarter_kernel(count, *refs):
    srcs, dsts = refs[:count], refs[count : 2 * count]
    sems = Sems(*refs[2 * count :])
    greet([tensor_place()[3], *swap_peers()])
    run(swap_plan(srcs, [lambda me, o=o: o.at[me] for o in dsts], sems))


def swap_quarters(collective_id, *arrays):
    n = len(arrays)
    return pl.pallas_call(
        functools.partial(quarter_kernel, n),
        out_shape=[jax.ShapeDtypeStruct(a.shape, a.dtype) for a in arrays],
        in_specs=vmem_specs(n),
        out_specs=vmem_specs(n),
        scratch_shapes=sem_pair(3 * n),
        compiler_params=params(collective_id),
        name="swap_quarters",
    )(*arrays)


CHUNKS = 4
HALF = ROWS // 2


def rows_plan(x, o, sems):
    d, c, m, core, across, copy_of = tensor_place()
    me, far = 2 * d + c, 2 * (1 - d) + c
    copies, firsts, seconds = [], [], []
    step = HALF // 2
    mine = [pl.ds(m * HALF + k * step, step) for k in range(2)]
    other = [pl.ds((1 - m) * HALF + k * step, step) for k in range(2)]
    for rows in mine:
        firsts.append(started(copies, x.at[rows], o.at[me, rows], *sems.take(), across))
    near = started(copies, x, o.at[me], *sems.take(), core)
    o[me] = x[...]
    yield
    for k, rows in enumerate(other):
        firsts[k].wait_recv()
        seconds.append(started(copies, o.at[far, rows], o.at[far, rows], *sems.take(), copy_of))
    yield
    lasts = []
    for rows in other:
        lasts.append(started(copies, o.at[far, rows], o.at[far, rows], *sems.take(), core))
    for k, rows in enumerate(mine):
        seconds[k].wait_recv()
        lasts.append(started(copies, o.at[far, rows], o.at[far, rows], *sems.take(), core))
    yield
    near.wait_recv()
    for copy in lasts:
        copy.wait_recv()
    for copy in copies:
        copy.wait_send()


ROWS_SEMS = 9


def rows_kernel(x, o, send, recv):
    greet(tensor_place()[3:])
    run(rows_plan(x, o, Sems(send, recv)))


def gather_rows(x):
    out = pl.pallas_call(
        rows_kernel,
        out_shape=jax.ShapeDtypeStruct((4, *x.shape), x.dtype),
        in_specs=vmem_specs(1),
        out_specs=vmem_specs(1)[0],
        scratch_shapes=sem_pair(ROWS_SEMS),
        compiler_params=params(1),
        name="gather_rows",
    )(x)
    return out.reshape(4 * x.shape[0], x.shape[1])


def sum_plan(x, o, buffers, sems):
    from_core, s_here, s_send, from_across, t_send, from_copy = buffers
    d, c, m, core, across, copy_of = tensor_place()
    step = ROWS // CHUNKS
    rows = [pl.ds(k * step, step) for k in range(CHUNKS)]
    copies, zero, one, two = [], [], [], []
    for r in rows:
        zero.append(started(copies, x.at[:, 1 - c, r], from_core.at[:, r], *sems.take(), core))
    yield
    for k, r in enumerate(rows):
        zero[k].wait_recv()
        s_send[r] = added(x[1 - d, c, r], from_core[1 - d, r]).astype(bf16)
        one.append(started(copies, s_send.at[r], from_across.at[r], *sems.take(), across))
        s_here[r] = added(x[d, c, r], from_core[d, r])
    yield
    for k, r in enumerate(rows):
        one[k].wait_recv()
        t_send[r] = added(s_here[r], from_across[r]).astype(bf16)
        two.append(started(copies, t_send.at[r], from_copy.at[r], *sems.take(), copy_of))
    yield
    for k, r in enumerate(rows):
        two[k].wait_recv()
        o[r] = added(t_send[r], from_copy[r])
    for copy in copies:
        copy.wait_send()


SUM_SEMS = 3 * CHUNKS
SUM_BUFFERS = [
    pltpu.VMEM((2, ROWS, D), bf16),
    pltpu.VMEM((ROWS, D), f32),
    pltpu.VMEM((ROWS, D), bf16),
    pltpu.VMEM((ROWS, D), bf16),
    pltpu.VMEM((ROWS, D), bf16),
    pltpu.VMEM((ROWS, D), bf16),
]


def sum_kernel(x, o, *scratch):
    greet(tensor_place()[3:])
    run(sum_plan(x, o, scratch[:6], Sems(*scratch[6:])))


def sum_rows(x):
    return pl.pallas_call(
        sum_kernel,
        out_shape=jax.ShapeDtypeStruct((ROWS, D), f32),
        in_specs=vmem_specs(1),
        out_specs=vmem_specs(1)[0],
        scratch_shapes=SUM_BUFFERS + sem_pair(SUM_SEMS),
        compiler_params=params(2),
        name="sum_rows",
    )(x.reshape(2, 2, ROWS, D))


def weights_plan(w, first, second, low, sems):
    i0, i_up, i_down, i_far, to_i_up, to_i_down = ring(first)
    j0, j_up, j_down, j_far, to_j_up, to_j_down = ring(second)

    def at(i, j, part, n):
        return w.at[(j, i) if first == "y" else (i, j)].at[pl.ds(low + part, n)]

    copies = []

    def send(ref, peer):
        return started(copies, ref, ref, *sems.take(), peer)

    def along(i):
        return i, send(at(i, j0, 0, 2), to_j_up), send(at(i, j0, 0, 2), to_j_down)

    from_down, from_up = send(at(i0, j0, 0, 2), to_i_up), send(at(i0, j0, 0, 2), to_i_down)
    second_leg = [along(i0)]
    yield
    from_down.wait_recv()
    far_low = send(at(i_down, j0, 0, 1), to_i_up)
    from_up.wait_recv()
    far_high = send(at(i_up, j0, 1, 1), to_i_down)
    second_leg += [along(i_down), along(i_up)]
    yield
    onward = []

    def relay(leg):
        i, a, b = leg
        a.wait_recv()
        onward.append(send(at(i, j_down, 0, 1), to_j_up))
        b.wait_recv()
        onward.append(send(at(i, j_up, 1, 1), to_j_down))

    relay(second_leg[0])
    yield
    far_low.wait_recv()
    far_high.wait_recv()
    second_leg.append(along(i_far))
    for leg in second_leg[1:]:
        yield
        relay(leg)
    yield
    for copy in onward:
        copy.wait_recv()
    for copy in copies:
        copy.wait_send()


WEIGHT_SEMS = 20


def start_kernel(first, second, third, x, w, s2, s3, rows, *sems):
    z, y = lax.axis_index("z"), lax.axis_index("y")
    _, _, _, _, z_up, z_down = ring("z")
    _, _, _, _, y_up, y_down = ring("y")
    greet([*tensor_place()[3:], *swap_peers(), z_up, z_down, y_up, y_down])
    one = Sems(*sems[:2])
    swap_first = swap_plan([first], [lambda me: w.at[z, y, me]], one)
    next(swap_first)
    gather_x = rows_plan(x, rows, Sems(*sems[2:4]))
    next(gather_x)
    swap_rest = swap_plan([second, third], [lambda me: s2.at[me], lambda me: s3.at[me]], one)
    next(swap_rest)
    next(swap_first)
    run(
        weights_plan(w, "y", "z", 0, Sems(*sems[4:6])),
        weights_plan(w, "z", "y", 2, Sems(*sems[6:8])),
        gather_x,
        swap_rest,
        swap_first,
    )


def start(first, second, third, x):
    return pl.pallas_call(
        start_kernel,
        out_shape=[
            jax.ShapeDtypeStruct((4, 4, *first.shape), bf16),
            jax.ShapeDtypeStruct(second.shape, bf16),
            jax.ShapeDtypeStruct(third.shape, bf16),
            jax.ShapeDtypeStruct((4, *x.shape), bf16),
        ],
        in_specs=vmem_specs(4),
        out_specs=vmem_specs(4),
        scratch_shapes=sem_pair(9) + sem_pair(ROWS_SEMS) + sem_pair(WEIGHT_SEMS) + sem_pair(WEIGHT_SEMS),
        compiler_params=params(3),
        name="start",
    )(first, second, third, x)


def spread_plan(x, q, kv, sems):
    z, z_up, z_down, z_far, to_z_up, to_z_down = ring("z")
    y, y_up, y_down, y_far, to_y_up, to_y_down = ring("y")
    far = {"z": z_far}
    copies, firsts, queries, nears, fars = [], [], [], [], []
    both = pl.ds(1, 2)
    peers = [(z_up, to_z_up, z_down), (z_down, to_z_down, z_up), (z_far, far, z_far)]
    for place, peer, _ in peers:
        firsts.append(started(copies, x.at[place, both], kv.at[z, y], *sems.take(), peer))
    kv[z, y] = x[z, both]

    def along(place):
        ref = kv.at[place, y]
        nears.append(
            (place, started(copies, ref, ref, *sems.take(), to_y_up), started(copies, ref, ref, *sems.take(), to_y_down))
        )

    along(z)
    for place, peer, _ in peers:
        queries.append(started(copies, x.at[place, 0], q.at[z], *sems.take(), peer))
    q[z] = x[z, 0]
    yield

    def relay(k):
        place, a, b = nears[k]
        a.wait_recv()
        ref = kv.at[place, y_down, 0]
        fars.append(started(copies, ref, ref, *sems.take(), to_y_up))
        b.wait_recv()
        ref = kv.at[place, y_up, 1]
        fars.append(started(copies, ref, ref, *sems.take(), to_y_down))

    for k, (_, _, source) in enumerate(peers):
        firsts[k].wait_recv()
        along(source)
        yield
        relay(k)
    yield
    relay(3)
    yield
    for copy in queries + fars:
        copy.wait_recv()
    for copy in copies:
        copy.wait_send()


def spread_kernel(x, cot, q, kv, rows, *sems):
    _, _, _, z_far, z_up, z_down = ring("z")
    _, _, _, _, y_up, y_down = ring("y")
    greet([*tensor_place()[3:], z_up, z_down, {"z": z_far}, y_up, y_down])
    run(spread_plan(x, q, kv, Sems(*sems[:2])), rows_plan(cot, rows, Sems(*sems[2:])))


def spread(x, cot):
    return pl.pallas_call(
        spread_kernel,
        out_shape=[
            jax.ShapeDtypeStruct((4, BLOCK, HD), bf16),
            jax.ShapeDtypeStruct((4, 4, 2, BLOCK, HD), bf16),
            jax.ShapeDtypeStruct((4, *cot.shape), bf16),
        ],
        in_specs=vmem_specs(2),
        out_specs=vmem_specs(3),
        scratch_shapes=sem_pair(22) + sem_pair(ROWS_SEMS),
        compiler_params=params(4),
        name="spread",
    )(x, cot)


def turn_kernel(x, o, send, recv):
    z, z_up, z_down, z_far, to_z_up, to_z_down = ring("z")
    peers = [(z_up, to_z_up), (z_down, to_z_down), (z_far, {"z": z_far})]
    greet([peer for _, peer in peers])
    sems, copies = Sems(send, recv), []
    for place, peer in peers:
        started(copies, x.at[place], o.at[z], *sems.take(), peer)
    o[z] = x[z]
    for copy in copies:
        copy.wait()


def turn(x):
    return pl.pallas_call(
        turn_kernel,
        out_shape=jax.ShapeDtypeStruct(x.shape, x.dtype),
        in_specs=vmem_specs(1),
        out_specs=vmem_specs(1)[0],
        scratch_shapes=sem_pair(3),
        compiler_params=params(5),
        name="turn",
    )(x)


def ring_sum(at, axis, buffers, sems, put):
    one, two, passed = buffers
    me, up, down, far, to_up, to_down = ring(axis)
    copies = []
    a = started(copies, at(far, 0), one.at[0], *sems.take(), to_up)
    b = started(copies, at(far, 1), one.at[1], *sems.take(), to_down)
    plain = [
        started(copies, at(up, 1), two.at[0, 1], *sems.take(), to_up),
        started(copies, at(down, 0), two.at[1, 0], *sems.take(), to_down),
    ]
    yield
    a.wait_recv()
    passed[0] = added(at(up, 0)[...], one[0]).astype(bf16)
    plain.append(started(copies, passed.at[0], two.at[0, 0], *sems.take(), to_up))
    b.wait_recv()
    passed[1] = added(at(down, 1)[...], one[1]).astype(bf16)
    plain.append(started(copies, passed.at[1], two.at[1, 1], *sems.take(), to_down))
    yield
    for copy in plain:
        copy.wait_recv()
    for part in range(2):
        put(part, added(at(me, part)[...], two[0, part], two[1, part]))
    yield
    for copy in copies:
        copy.wait_send()


RING_SEMS = 6


def ring_buffers(n, part):
    return [pltpu.VMEM((n, 2, *part), bf16), pltpu.VMEM((n, 2, 2, *part), bf16), pltpu.VMEM((n, 2, *part), bf16)]


def collect_plan(dq, dkv, o, total, buffers, sems):
    z, z_up, z_down, z_far, to_z_up, to_z_down = ring("z")
    y = lax.axis_index("y")
    peers = [(z_up, to_z_up), (z_down, to_z_down), (z_far, {"z": z_far}), (z, None)]
    copies, rings = [], []
    for k, (place, peer) in enumerate(peers):

        def at(i, part, place=place):
            return dkv.at[place, i, part]

        def put(part, value, k=k):
            if k < 3:
                total[k, part] = value.astype(bf16)
            else:
                o[z, 1 + part] = value.astype(bf16)

        rings.append(ring_sum(at, "y", [b.at[k] for b in buffers], sems, put))
    for r in rings:
        next(r)
    for place, peer in peers[:3]:
        started(copies, dq.at[place], o.at[z, 0], *sems.take(), peer)
    o[z, 0] = dq[z]
    yield
    for r in rings:
        next(r)
        yield
    for k, r in enumerate(rings):
        next(r)
        if k < 3:
            started(copies, total.at[k], o.at[z, pl.ds(1, 2)], *sems.take(), peers[k][1])
        yield
    for copy in copies:
        copy.wait()
    run(*rings)


def collect_kernel(dq, dkv, part, o, summed, total, *scratch):
    _, _, _, z_far, z_up, z_down = ring("z")
    _, _, _, _, y_up, y_down = ring("y")
    greet([*tensor_place()[3:], z_up, z_down, {"z": z_far}, y_up, y_down])
    run(
        collect_plan(dq, dkv, o, total, scratch[:3], Sems(*scratch[3:5])),
        sum_plan(part, summed, scratch[5:11], Sems(*scratch[11:])),
    )


def collect(dq, dkv, part):
    return pl.pallas_call(
        collect_kernel,
        out_shape=[jax.ShapeDtypeStruct((4, 3, BLOCK, HD), bf16), jax.ShapeDtypeStruct((ROWS, D), f32)],
        in_specs=vmem_specs(3),
        out_specs=vmem_specs(2),
        scratch_shapes=[pltpu.VMEM((3, 2, BLOCK, HD), bf16)]
        + ring_buffers(4, (BLOCK, HD))
        + sem_pair(4 * RING_SEMS + 6)
        + SUM_BUFFERS
        + sem_pair(SUM_SEMS),
        compiler_params=params(6),
        name="collect",
    )(dq, dkv, part.reshape(2, 2, ROWS, D))


def grads_plan(g, shard, first, second, low, legs, buffers, sems):
    rings = []
    for j in range(4):

        def at(i, part, j=j):
            return g.at[(j, i) if first == "y" else (i, j)].at[low + part]

        def put(part, value, j=j):
            legs[j, part] = value.astype(bf16)

        rings.append(ring_sum(at, first, [b.at[j] for b in buffers], sems, put))
    for r in rings:
        next(r)
    yield
    for r in rings:
        next(r)
    yield
    for r in rings:
        next(r)

    def put_last(part, value):
        shard[low + part] = value.astype(bf16)

    rings.append(ring_sum(lambda i, part: legs.at[i, part], second, [b.at[4] for b in buffers], sems, put_last))
    for _ in range(3):
        next(rings[-1])
        yield
    run(*rings)


def end_kernel(wide, g, part, o, gain, summed, *scratch):
    d, c, m, core, across, copy_of = tensor_place()
    _, _, _, _, z_up, z_down = ring("z")
    _, _, _, _, y_up, y_down = ring("y")
    greet([core, across, copy_of, *swap_peers(), z_up, z_down, y_up, y_down])
    shard, mine, theirs, legs_a, legs_b = scratch[:5]
    scratch = scratch[5:]
    run(
        sum_plan(part, summed, scratch[6:12], Sems(*scratch[12:14])),
        grads_plan(g, shard, "z", "y", 0, legs_a, scratch[:3], Sems(*scratch[14:16])),
        grads_plan(g, shard, "y", "z", 2, legs_b, scratch[3:6], Sems(*scratch[16:18])),
    )
    last = Sems(*scratch[18:])
    run(swap_plan([shard], [lambda me: o.at[me]], last))
    lanes = pl.ds(wide, HD)
    mine[...] = added(o[0, :, lanes], o[1, :, lanes], o[2, :, lanes], o[3, :, lanes])
    copy = remote(mine, theirs, *last.take(), copy_of)
    copy.start()
    copy.wait()
    gain[...] = mine[...] + theirs[...]


def end(g, part):
    block = (32, g.shape[1])
    return pl.pallas_call(
        functools.partial(end_kernel, g.shape[1] - HD),
        out_shape=[
            jax.ShapeDtypeStruct((4, *block), bf16),
            jax.ShapeDtypeStruct((32, HD), f32),
            jax.ShapeDtypeStruct((ROWS, D), f32),
        ],
        in_specs=vmem_specs(2),
        out_specs=vmem_specs(3),
        scratch_shapes=[
            pltpu.VMEM((4, *block), bf16),
            pltpu.VMEM((32, HD), f32),
            pltpu.VMEM((32, HD), f32),
            pltpu.VMEM((4, 2, *block), bf16),
            pltpu.VMEM((4, 2, *block), bf16),
        ]
        + ring_buffers(5, block)
        + ring_buffers(5, block)
        + SUM_BUFFERS
        + sem_pair(SUM_SEMS)
        + sem_pair(5 * RING_SEMS)
        + sem_pair(5 * RING_SEMS)
        + sem_pair(4),
        compiler_params=params(7),
        name="end",
    )(g.reshape(4, 4, 4, *block), part.reshape(2, 2, ROWS, D))


def reach(info, block):
    t = block * BLOCK + lax.broadcasted_iota(jnp.int32, (BLOCK, 1), 0)
    begin = jnp.where(t >= info[2], info[2], jnp.where(t >= info[1], info[1], info[0]))
    end = jnp.minimum((t // FRAME + 1) * FRAME, info[3])
    living = t < info[3]
    return jnp.where(living, begin, t), jnp.where(living, end, t + 1)


def dot_t(a, b):
    return lax.dot_general(a, b, (((1,), (1,)), ((), ())), preferred_element_type=f32)


def dot_l(a, b):
    return lax.dot_general(a, b, (((0,), (0,)), ((), ())), preferred_element_type=f32)


def visible_scores(q, k, j, low, high):
    s = dot_t(q, k) * scale
    at = j * BLOCK + lax.broadcasted_iota(jnp.int32, (1, BLOCK), 1)
    return jnp.where((at >= low) & (at < high), s, -1e30)


def attend_kernel(info, q_ref, kv_ref, o_ref, lse_ref):
    block = 4 * pl.program_id(0) + info[4]
    low, high = reach(info, block)
    q = q_ref[0]

    def step(j, state):
        top, total, acc = state
        s = visible_scores(q, kv_ref[j, 0], j, low, high)
        now = jnp.maximum(top, jnp.max(s, -1, keepdims=True))
        p = jnp.exp(s - now)
        shrink = jnp.exp(top - now)
        total = total * shrink + jnp.sum(p, -1, keepdims=True)
        acc = acc * shrink + jnp.dot(p.astype(bf16), kv_ref[j, 1], preferred_element_type=f32)
        return now, total, acc

    top, total, acc = lax.fori_loop(
        0,
        block + 1,
        step,
        (jnp.full((BLOCK, 1), -1e30, f32), jnp.zeros((BLOCK, 1), f32), jnp.zeros((BLOCK, HD), f32)),
    )
    o_ref[0] = acc / total
    lse_ref[0] = jnp.broadcast_to(top + jnp.log(total), (BLOCK, HD))


def attend(info, q, kv):
    return pl.pallas_call(
        attend_kernel,
        grid=(4,),
        out_shape=[jax.ShapeDtypeStruct((4, BLOCK, HD), f32)] * 2,
        in_specs=[
            pl.BlockSpec(memory_space=pltpu.SMEM),
            pl.BlockSpec((1, BLOCK, HD), lambda i: (i, 0, 0)),
            pl.BlockSpec((16, 2, BLOCK, HD), lambda i: (0, 0, 0, 0)),
        ],
        out_specs=[pl.BlockSpec((1, BLOCK, HD), lambda i: (i, 0, 0))] * 2,
        compiler_params=params(),
        cost_estimate=pl.CostEstimate(flops=20 * 10**9, bytes_accessed=4 * 10**6, transcendentals=10**6),
        name="attend",
    )(info, q, kv.reshape(16, 2, BLOCK, HD))


def attend_back_kernel(info, q_ref, kv_ref, o_ref, lse_ref, do_ref, dq_ref, dkv_ref, acc):
    i = pl.program_id(0)
    block = 4 * i + info[4]
    low, high = reach(info, block)
    q, do = q_ref[0], do_ref[0]
    lse = lse_ref[0][:, :1]
    inner = jnp.sum(o_ref[0] * do.astype(f32), -1, keepdims=True)

    @pl.when(i == 0)
    def _():
        acc[...] = jnp.zeros_like(acc)

    def step(j, dq):
        k, v = kv_ref[j, 0], kv_ref[j, 1]
        p = jnp.exp(visible_scores(q, k, j, low, high) - lse)
        acc[j, 1] += dot_l(p.astype(bf16), do)
        ds = (p * (dot_t(do, v) - inner)).astype(bf16)
        acc[j, 0] += dot_l(ds, q)
        return dq + jnp.dot(ds, k, preferred_element_type=f32)

    dq = lax.fori_loop(0, block + 1, step, jnp.zeros((BLOCK, HD), f32))
    dq_ref[0] = (dq * scale).astype(bf16)

    @pl.when(i == 3)
    def _():
        def cast(j, _):
            dkv_ref[j, 0] = (acc[j, 0] * scale).astype(bf16)
            dkv_ref[j, 1] = acc[j, 1].astype(bf16)
            return 0

        lax.fori_loop(0, 16, cast, 0)


def attend_back(info, q, kv, o, lse, do):
    dq, dkv = pl.pallas_call(
        attend_back_kernel,
        grid=(4,),
        out_shape=[
            jax.ShapeDtypeStruct((4, BLOCK, HD), bf16),
            jax.ShapeDtypeStruct((16, 2, BLOCK, HD), bf16),
        ],
        in_specs=[
            pl.BlockSpec(memory_space=pltpu.SMEM),
            pl.BlockSpec((1, BLOCK, HD), lambda i: (i, 0, 0)),
            pl.BlockSpec((16, 2, BLOCK, HD), lambda i: (0, 0, 0, 0)),
        ]
        + [pl.BlockSpec((1, BLOCK, HD), lambda i: (i, 0, 0))] * 3,
        out_specs=[
            pl.BlockSpec((1, BLOCK, HD), lambda i: (i, 0, 0)),
            pl.BlockSpec((16, 2, BLOCK, HD), lambda i: (0, 0, 0, 0)),
        ],
        scratch_shapes=[pltpu.VMEM((16, 2, BLOCK, HD), f32)],
        compiler_params=params(),
        cost_estimate=pl.CostEstimate(flops=30 * 10**9, bytes_accessed=8 * 10**6, transcendentals=10**6),
        name="attend_back",
    )(info, q, kv.reshape(16, 2, BLOCK, HD), o, lse, do)
    return dq, dkv.reshape(4, 4, 2, BLOCK, HD)


def to_inner(x):
    return x.reshape(-1, 2, 16, 64).swapaxes(1, 2).reshape(-1, D)


def to_outer(x):
    return x.reshape(-1, 16, 2, 64).swapaxes(1, 2).reshape(-1, D)


def norm(value):
    centre = value - jnp.mean(value, -1, keepdims=True)
    r = lax.rsqrt(jnp.mean(centre * centre, -1, keepdims=True) + epsilon)
    return centre * r, r


def norm_back(grad, n, r, gain):
    e = grad * gain
    return r * (e - jnp.mean(e, -1, keepdims=True) - n * jnp.mean(e * n, -1, keepdims=True))


def turned(x, cosine, sine, direction):
    a, b = x[..., :64], x[..., 64:]
    return jnp.concatenate([a * cosine - direction * b * sine, direction * a * sine + b * cosine], -1)


def quarters(w):
    return w.reshape(w.shape[0], 4, -1).swapaxes(0, 1)


def joined(w):
    return w.swapaxes(0, 1).reshape(w.shape[1], -1)


def gelu(v):
    return jax.nn.gelu(v, approximate=False)


def gather_weights(x):
    return lax.all_gather(x, ZY, axis=0, tiled=True)


def scatter_grads(x):
    return lax.psum_scatter(x, ZY, scatter_dimension=0, tiled=True)


def local(
    inputs,
    clip_starts,
    pad_lengths,
    w_query,
    w_key,
    w_value,
    w_out,
    w_up,
    w_down,
    gain_first,
    gain_second,
    cotangent,
):
    z, y = lax.axis_index("z"), lax.axis_index("y")
    living = LEN - pad_lengths
    side = jnp.concatenate(
        [
            gain_first[:, None],
            gain_second[:, None],
            jnp.broadcast_to(clip_starts, (32, 3)).astype(bf16),
            jnp.broadcast_to(pad_lengths[None], (32, 1)).astype(bf16),
            jnp.zeros((32, HD - 6), bf16),
        ],
        1,
    )
    first = jnp.concatenate(
        [quarters(w_query), quarters(w_key), quarters(w_value), jnp.broadcast_to(side, (4, 32, HD))], -1
    )
    second = jnp.concatenate([quarters(w_out.T), quarters(w_up)], -1)
    third = quarters(w_down.T)
    x_here = to_inner(inputs[0])
    first, second, third, x_all = start(first, second, third, x_here)
    first = first.reshape(D, -1)
    second = gather_weights(second.reshape(HD, -1))
    down = gather_weights(third.reshape(HD, -1))

    side = first[:, 768:]
    gains = side[:, :2].astype(f32).T
    gain_one, gain_two = gains[0], gains[1]
    facts = side[:128:64, 2:6].astype(jnp.int32)
    begins, ends = facts[:, :3], LEN - facts[:, 3]

    n_all, _ = norm(x_all.reshape(512, D).astype(f32))
    normed_one = (n_all * gain_one).astype(bf16)
    incoming = to_inner(cotangent[0])

    places = (4 * z + y) * BLOCK + jnp.arange(BLOCK, dtype=jnp.int32)
    opened = begins[:, None, :] <= places[None, :, None]
    position = places - jnp.max(jnp.where(opened, begins[:, None, :], 0), -1)
    frequency = 10000.0 ** (-2.0 * jnp.arange(HD // 2, dtype=f32) / HD)
    angles = position.astype(f32)[..., None] * frequency
    cosine, sine = jnp.cos(angles)[:, :, None], jnp.sin(angles)[:, :, None]

    lin = jnp.dot(normed_one, first, preferred_element_type=f32)
    lin = lin[:, :768].reshape(2, BLOCK, 3, 2, HD)
    query = turned(lin[:, :, 0], cosine, sine, 1.0)
    key = turned(lin[:, :, 1], cosine, sine, 1.0)
    qkv = jnp.stack([query, key, lin[:, :, 2]], 0).astype(bf16)
    qkv = qkv.transpose(1, 3, 0, 2, 4).reshape(4, 3, BLOCK, HD)
    q, kv, incoming_all = spread(qkv, incoming)
    incoming_all = incoming_all.reshape(512, D)
    mine = z // 2
    info = jnp.concatenate(
        [lax.dynamic_index_in_dim(begins, mine, 0, False), lax.dynamic_index_in_dim(ends, mine, 0), y[None]]
    ).astype(jnp.int32)
    o, lse = attend(info, q, kv)
    mixed = turn(o.astype(bf16))
    mixed = mixed.reshape(2, 2, BLOCK, HD).swapaxes(1, 2).reshape(512, 2 * HD)

    x = x_here.astype(f32)
    out = second[:, :256]
    middle = x + sum_rows(dot_t(mixed, out).astype(bf16))
    n_two, r_two = norm(middle)
    normed_two = gather_rows((n_two * gain_two).astype(bf16))
    hidden = jnp.dot(normed_two, second, preferred_element_type=f32)[:, 256:]
    active, pull = jax.vjp(gelu, hidden)
    active = active.astype(bf16)
    grad_active = jnp.dot(incoming_all, down, preferred_element_type=f32)
    grad_hidden = pull(grad_active)[0].astype(bf16)
    part_two = dot_t(jnp.pad(grad_hidden, ((0, 0), (256, 0))), second).astype(bf16)
    feed = jnp.concatenate(
        [dot_l(incoming_all, active).astype(bf16), dot_l(normed_two, grad_hidden).astype(bf16)], 1
    )
    part_two, feed = lax.optimization_barrier((part_two, feed))
    feed = scatter_grads(feed)
    grad_normed_two = sum_rows(part_two)
    grad_middle = incoming.astype(f32) + norm_back(grad_normed_two, n_two, r_two, gain_two)
    branch = gather_rows(grad_middle.astype(bf16))

    grad_mixed = jnp.dot(branch, out, preferred_element_type=f32).astype(bf16)
    grad_mixed = grad_mixed.reshape(2, BLOCK, 2, HD).swapaxes(1, 2).reshape(4, BLOCK, HD)
    dq, dkv = attend_back(info, q, kv, o, lse, turn(grad_mixed))
    grads, fed = collect(dq, dkv, dot_t(active, down).astype(bf16))
    output = middle + fed
    grads = grads.reshape(2, 2, 3, BLOCK, HD).transpose(2, 0, 3, 1, 4)
    grad_query = turned(grads[0].astype(f32), cosine, sine, -1.0).astype(bf16)
    grad_key = turned(grads[1].astype(f32), cosine, sine, -1.0).astype(bf16)
    grad_lin = jnp.stack([grad_query, grad_key, grads[2]], 2).reshape(512, 768)

    part_one = dot_t(jnp.pad(grad_lin, ((0, 0), (0, HD))), first)
    gain_grads = jnp.stack([jnp.sum(part_one * n_all, 0), 0.5 * jnp.sum(grad_normed_two * n_two, 0)], 1)
    last = jnp.concatenate(
        [
            dot_l(normed_one, grad_lin).astype(bf16),
            dot_l(branch, mixed).astype(bf16),
            jnp.pad(gain_grads, ((0, 0), (0, HD - 2))).astype(bf16),
        ],
        1,
    )
    last, gain_grads, grad_normed_one = end(last, part_one.astype(bf16))
    n_one, r_one = norm(x)
    grad_input = grad_middle + norm_back(grad_normed_one, n_one, r_one, gain_one)
    feed = swap_quarters(8, feed.reshape(4, 32, -1))[0].astype(f32)
    last = last.astype(f32)
    return (
        to_outer(output).astype(bf16)[None],
        to_outer(grad_input)[None],
        joined(last[:, :, :256]),
        joined(last[:, :, 256:512]),
        joined(last[:, :, 512:768]),
        joined(last[:, :, 768:1024]).T,
        joined(feed[:, :, 1024:]),
        joined(feed[:, :, :1024]).T,
        gain_grads[:, 0],
        gain_grads[:, 1],
    )


def solution(mesh):
    split = Mesh(mesh.devices.reshape(2, 4, 4, 2, 2), ("dp", "z", "y", "c", "mp"))
    seq = ("z", "y", "c")
    weights = ("dp", "z", "y", "c")
    tokens = P("dp", seq, None)
    wide, tall = P(weights, "mp"), P("mp", weights)
    return jax.shard_map(
        local,
        mesh=split,
        in_specs=(tokens, P("dp", None), P("dp"), wide, wide, wide, tall, wide, tall, P(weights), P(weights), tokens),
        out_specs=(tokens, tokens, wide, wide, wide, tall, wide, tall, P(weights), P(weights)),
        check_vma=False,
    )
```

time: 746 us -> 493 us (0.66)
  waiting for transfers between devices: 278 us -> 0.73 us
  local copies, waits for them, and re-layouts: 58 us -> 72.9 us
  other arithmetic: 22.6 us -> 34.7 us
    reduce_scatter x4 -> x1, waiting for transfers between devices: 241 us -> 0.01 us  [scatter_grads(): return lax.psum_scatter(x, ZY, scatter_dimension=0, tiled=True)]
    pallas_call x5, Pallas kernels: 124 us -> 176 us  [the longest x1 46.5 us: end(): pl.pallas_call(functools.partial(end_kernel, g.shape[1] - HD), out_shape=...]
    pallas_call x4 -> x2, Pallas kernels: 67.8 us -> 31.4 us  [gather_rows(): pl.pallas_call(rows_kernel, out_shape=jax.ShapeDtypeStruct((4, *x.shape),...]
    all_gather x3 -> x2, waiting for transfers between devices: 35.3 us -> 0.01 us  [gather_weights(): return lax.all_gather(x, ZY, axis=0, tiled=True)]
    pallas_call x2 -> x1, Pallas kernels: 30.3 us -> 10.3 us  [swap_quarters(): pl.pallas_call(functools.partial(quarter_kernel, n), out_shape=[jax.Shape...]
    concatenate x1 -> x2, other arithmetic: 2.04 us -> 10.8 us  [the longest x1 8.35 us: local(): jnp.concatenate([dot_l(incoming_all, active).astype(bf16), dot_l(normed_t...]
    unnamed x77 -> x80, local copies, waits for them, and re-layouts: 30.2 us -> 35.9 us
  transfers between devices with their start and end apart: 7 -> 3, of which waited for: 5 -> 0; matrix products, arithmetic and copies ran while one was open for 11% -> 20% of each run, Pallas kernels for 22% -> 53%
where the time goes in v2:
time: 493 us; the launch traced here: 487 us
  Pallas kernels  310 us (63%)
  local copies, waits for them, and re-layouts  72.9 us (15%)
  matrix products  53 us (11%)
  other arithmetic  34.7 us (7%)
  between operations  15.8 us (3%)
    pallas_call x1, Pallas kernels, end(): pl.pallas_call(functools.partial(end_kernel, g.shape[1] - HD), out_shape=...  46.5 us
    pallas_call x2, Pallas kernels, sum_rows(): pl.pallas_call(sum_kernel, out_shape=jax.ShapeDtypeStruct((ROWS, D), f32)...  43.8 us
    pallas_call x1, Pallas kernels, collect(): pl.pallas_call(collect_kernel, out_shape=[jax.ShapeDtypeStruct((4, 3, BLO...  43 us
    pallas_call x1, Pallas kernels, start(): pl.pallas_call(start_kernel, out_shape=[jax.ShapeDtypeStruct((4, 4, *firs...  42.8 us
    pallas_call x1, Pallas kernels, spread(): pl.pallas_call(spread_kernel, out_shape=[jax.ShapeDtypeStruct((4, BLOCK,...  37.8 us
    unnamed x80, local copies, waits for them, and re-layouts  35.9 us
    pallas_call x2, Pallas kernels, gather_rows(): pl.pallas_call(rows_kernel, out_shape=jax.ShapeDtypeStruct((4, *x.shape),...  31.4 us
    pallas_call x1, Pallas kernels, attend_back(): pl.pallas_call(attend_back_kernel, grid=(4,), out_shape=[jax.ShapeDtypeSt...  22.9 us
  transfers between devices with their start and end apart: 3, of which 0 were waited for; matrix products, arithmetic and copies ran while one was open for 20% of the time, Pallas kernels for 53%

profile of v2, /device:TPU:1, one launch (start us, length us, event | category | flops | bytes accessed | tf_op | source)
XLA Modules:
  0.0 486.9 jit_solution(1644397418383801818)
XLA Ops:
  15.9 42.8 %start.1 = (bf16[4,4,4,32,896]{4,3,2,1,0:T(8,128)(2,1)}, bf16[4,32,1280]{2,1,0:T(8,128)(2,1)}, bf16[4,32,1024]{2,1,0:T(8,128)(2,1)}, bf16[4,128,2048]{2,1,0:T(8,128)(2,1)S(1)}) custom-call(bf16[4,32,896]{2,1,0:T(8,128)(2,1)S(1)} %pad_maximum_fusion.4.first, bf16[4,32,1280]{2,1,0:T(8,128)(2,1)S(1)} %pad_maximum_fusion.3.second, ...), custom_call_target="tpu_custom_call" | custom-call | tf_op jit(solution)/shard_map/start/pallas_call | solution.py:323
  71.2 3.4 reshape.381
  92.7 37.8 %spread.1 = (bf16[4,256,128]{2,1,0:T(8,128)(2,1)S(1)}, bf16[4,4,2,256,128]{4,3,2,1,0:T(8,128)(2,1)S(1)}, bf16[4,128,2048]{2,1,0:T(8,128)(2,1)S(1)}) custom-call(bf16[4,3,256,128]{3,2,1,0:T(8,128)(2,1)S(1)} %bitcast.197, bf16[128,2048]{1,0:T(8,128)(2,1)S(1)} %copy.137.cot), custom_call_target="tpu_custom_call" | custom-call | tf_op jit(solution)/shard_map/spread/pallas_call | solution.py:393
  131.9 14.1 %attend.1 = (f32[4,256,128]{2,1,0:T(8,128)S(1)}, f32[4,256,128]{2,1,0:T(8,128)S(1)}) custom-call(s32[5]{0:T(128)S(1)} %pad_add_fusion.info, bf16[4,256,128]{2,1,0:T(8,128)(2,1)S(1)} %get-tuple-element.30.q_ref, bf16[16,2,256,128]{3,2,1,0:T(8,128)(2,1)S(1)} %bitcast.210), custom_call_target="tpu_custom_call" | custom-call | flops 20000000000 | bytes 4000000 | tf_op jit(solution)/shard_map/attend/pallas_call | solution.py:658
  146.9 7.9 %turn.2 = bf16[4,256,128]{2,1,0:T(8,128)(2,1)S(1)} custom-call(bf16[4,256,128]{2,1,0:T(8,128)(2,1)S(1)} %convert_element_type.166.x), custom_call_target="tpu_custom_call" | custom-call | tf_op jit(solution)/shard_map/turn/pallas_call | solution.py:421
  157.9 24.2 %sum_rows.2 = f32[128,2048]{1,0:T(8,128)S(1)} custom-call(bf16[2,2,128,2048]{3,2,1,0:T(8,128)(2,1)S(1)} %bitcast.196), custom_call_target="tpu_custom_call" | custom-call | tf_op jit(solution)/shard_map/sum_rows/pallas_call | solution.py:238
  183.4 15.6 %gather_rows.2 = bf16[4,128,2048]{2,1,0:T(8,128)(2,1)S(1)} custom-call(bf16[128,2048]{1,0:T(8,128)(2,1)S(1)} %multiply_convert_fusion.2.x), custom_call_target="tpu_custom_call" | custom-call | tf_op jit(solution)/shard_map/gather_rows/pallas_call | solution.py:182
  199.1 8.1 %multiply_convert_fusion.1 = (bf16[512,1024]{1,0:T(8,128)(2,1)S(1)}, f32[512,1024]{1,0:T(8,128)}, f32[512,1024]{1,0:T(8,128)}) fusion(bf16[512,2048]{1,0:T(8,128)(2,1)S(1)} %bitcast.200, bf16[2048,1280]{1,0:T(8,128)(2,1)S(1)} %bitcast.245), kind=kOutput, calls=%fused_computation.22 | convolution fusion | flops 2181562368 | bytes 11534336 | tf_op jit(solution)/shard_map/dot_general | solution.py:852
  208.1 4.3 convolution_convert_fusion.1
  212.5 7.0 %add_convert_fusion = bf16[512,1024]{1,0:T(8,128)(2,1)S(1)} fusion(f32[512,1024]{1,0:T(8,128)} %get-tuple-element.86, f32[512,1024]{1,0:T(8,128)} %get-tuple-element.123, bf16[512,2048]{1,0:T(8,128)(2,1)} %bitcast.212, bf16[2048,1024]{1,0:T(8,128)(2,1)} %all-gather.5.cloned.1.call-done), kind=kOutput, calls=%fused_computation.23 | convolution fusion | flops 2154823680 | bytes 11534336 | tf_op jit(solution)/shard_map/dot_general | solution.py:855
  220.5 4.4 convolution_convert_fusion
  224.9 8.4 %pad_maximum_fusion = bf16[2048,2048]{0,1:T(8,128)(2,1)} fusion(bf16[2048,1024]{0,1:T(8,128)(2,1)} %convolution_convert_fusion, bf16[2048,1024]{0,1:T(8,128)(2,1)} %convolution_convert_fusion.1), kind=kLoop, calls=%fused_computation | loop fusion | flops 16777216 | bytes 16777216 | tf_op jit(solution)/shard_map/concatenate | solution.py:858
  233.2 7.1 %convolution_convert_fusion.5 = bf16[512,2048]{1,0:T(8,128)(2,1)} fusion(bf16[2048,1280]{1,0:T(8,128)(2,1)} %all-gather.3.cloned.1.call-done, bf16[512,1024]{1,0:T(8,128)(2,1)} %copy-done.32), kind=kOutput, calls=%fused_computation.19 | convolution fusion | flops 2685403136 | bytes 8388608 | tf_op jit(solution)/shard_map/dot_general | solution.py:619
  240.3 12.6 %copy.158 = bf16[2048,2048]{1,0:T(8,128)(2,1)} copy(bf16[2048,2048]{0,1:T(8,128)(2,1)} %pad_maximum_fusion) | data formatting | bytes 16777216
  257.3 19.6 %sum_rows.3 = f32[128,2048]{1,0:T(8,128)S(1)} custom-call(bf16[2,2,128,2048]{3,2,1,0:T(8,128)(2,1)S(1)} %bitcast.202), custom_call_target="tpu_custom_call" | custom-call | tf_op jit(solution)/shard_map/sum_rows/pallas_call | solution.py:238
  278.8 15.8 %gather_rows.3 = bf16[4,128,2048]{2,1,0:T(8,128)(2,1)S(1)} custom-call(bf16[128,2048]{1,0:T(8,128)(2,1)S(1)} %get-tuple-element.83.x), custom_call_target="tpu_custom_call" | custom-call | tf_op jit(solution)/shard_map/gather_rows/pallas_call | solution.py:182
  298.1 9.3 %turn.3.do_ref = bf16[4,256,128]{2,1,0:T(8,128)(2,1)S(1)} custom-call(bf16[4,256,128]{2,1,0:T(8,128)(2,1)S(1)} %bitcast.206), custom_call_target="tpu_custom_call" | custom-call | tf_op jit(solution)/shard_map/turn/pallas_call | solution.py:421
  307.4 6.4 %convolution_convert_fusion.3 = bf16[512,2048]{1,0:T(8,128)(2,1)} fusion(bf16[512,1024]{1,0:T(8,128)(2,1)} %copy-done.31, bf16[2048,1024]{1,0:T(8,128)(2,1)} %all-gather.5.cloned.1.call-done), kind=kOutput, calls=%fused_computation.17 | convolution fusion | flops 2148532224 | bytes 7340032 | tf_op jit(solution)/shard_map/dot_general | solution.py:619
  313.9 22.9 %attend_back.1 = (bf16[4,256,128]{2,1,0:T(8,128)(2,1)S(1)}, bf16[16,2,256,128]{3,2,1,0:T(8,128)(2,1)S(1)}) custom-call(s32[5]{0:T(128)S(1)} %pad_add_fusion.info, bf16[4,256,128]{2,1,0:T(8,128)(2,1)S(1)} %get-tuple-element.30.q_ref, bf16[16,2,256,128]{3,2,1,0:T(8,128)(2,1)S(1)} %bitcast.211, f32[4,256,128]{2,1,0:T(8,128)S(1)} %copy-done.8, ...), custom_call_target="tpu_custom_call" | custom-call | flops 30000001024 | bytes 8000000 | tf_op jit(solution)/shard_map/attend_back/pallas_call | solution.py:708
  336.8 43.0 %collect.1 = (bf16[4,3,256,128]{3,2,1,0:T(8,128)(2,1)S(1)}, f32[128,2048]{1,0:T(8,128)S(1)}) custom-call(bf16[4,256,128]{2,1,0:T(8,128)(2,1)S(1)} %get-tuple-element.38.dq, bf16[4,4,2,256,128]{4,3,2,1,0:T(8,128)(2,1)S(1)} %bitcast.204, bf16[2,2,128,2048]{3,2,1,0:T(8,128)(2,1)} %bitcast.225), custom_call_target="tpu_custom_call" | custom-call | tf_op jit(solution)/shard_map/collect/pallas_call | solution.py:513
  393.8 6.1 %fusion.49 = (bf16[512,2048]{1,0:T(8,128)(2,1)}, bf16[2048]{0:T(1024)(128)(2,1)S(1)}) fusion(f32[512]{0:T(512)S(1)} %get-tuple-element.121, f32[512]{0:T(512)S(1)} %get-tuple-element.119, bf16[4,128,2048]{2,1,0:T(8,128)(2,1)S(1)} %get-tuple-element.29, bf16[2048,896]{1,0:T(8,128)(2,1)} %bitcast.238, bf16[512,768]{1,0:T(8,128)(2,1)} %reshape.399), kind=kOutput, calls=%fused_computation.148 | convolution fusion | flops 1885337600 | bytes 8658944 | tf_op jit(solution)/shard_map/dot_general | solution.py:619
  406.1 7.1 %copy.146 = bf16[2048,1152]{1,0:T(8,128)(2,1)} copy(bf16[2048,1152]{0,1:T(8,128)(2,1)} %pad_maximum_fusion.1) | data formatting | bytes 9437184 | tf_op jit(solution)/shard_map/concatenate | solution.py:879
  413.3 46.5 %end.1 = (bf16[4,32,1152]{2,1,0:T(8,128)(2,1)S(1)}, f32[32,128]{1,0:T(8,128)S(1)}, f32[128,2048]{1,0:T(8,128)S(1)}) custom-call(bf16[4,4,4,32,1152]{4,3,2,1,0:T(8,128)(2,1)} %bitcast.214, bf16[2,2,128,2048]{3,2,1,0:T(8,128)(2,1)S(1)} %bitcast.203), custom_call_target="tpu_custom_call" | custom-call | tf_op jit(solution)/shard_map/end/pallas_call | solution.py:582
  467.7 10.3 %swap_quarters.1 = bf16[4,32,2048]{2,1,0:T(8,128)(2,1)S(1)} custom-call(bf16[4,32,2048]{2,1,0:T(8,128)(2,1)S(1)} %bitcast.209), custom_call_target="tpu_custom_call" | custom-call | tf_op jit(solution)/shard_map/swap_quarters/pallas_call | solution.py:128
  (187 shorter events, 86.6 us)
Async XLA Ops:
  7.2 148.6 %all-gather.3.cloned.1.call-start = ((), (), s32[]{:S(2)}) async-start(), calls=%async_computation.1 | async-start | bytes 5570560 | tf_op jit(solution)/shard_map/all_gather | solution.py:770
  11.7 3.6 copy-start.29
  11.7 3.6 copy-start.30
  58.6 153.8 %all-gather.5.cloned.1.call-start = ((), (), s32[]{:S(2)}) async-start(), calls=%async_computation.2 | async-start | bytes 4456448 | tf_op jit(solution)/shard_map/all_gather | solution.py:770
  59.4 407.3 %reduce-scatter.4.cloned.1.call-start = ((), (), s32[]{:S(2)}) async-start(), calls=%async_computation.3 | async-start | bytes 8912896 | tf_op jit(solution)/shard_map/reduce_scatter | solution.py:774
  65.5 2.8 copy-start.28
  84.4 2.3 copy-start.21
  130.6 15.5 %copy-start.10 = (bf16[4,4,2,256,128]{4,3,2,1,0:T(8,128)(2,1)}, bf16[4,4,2,256,128]{4,3,2,1,0:T(8,128)(2,1)S(1)}, u32[]{:S(2)}) copy-start(bf16[4,4,2,256,128]{4,3,2,1,0:T(8,128)(2,1)S(1)} %get-tuple-element.31) | copy-start | bytes 6291460
  146.9 7.9 %copy-start.7 = (f32[4,256,128]{2,1,0:T(8,128)}, f32[4,256,128]{2,1,0:T(8,128)S(1)}, u32[]{:S(2)}) copy-start(f32[4,256,128]{2,1,0:T(8,128)S(1)} %get-tuple-element.32.o_ref) | copy-start | bytes 1572868
  157.8 41.2 %slice-start = ((s8[5242880]{0:T(1024)(128)(4,1)}), s8[4194304]{0:T(1024)(128)(4,1)S(1)}, s32[]{:S(2)}) async-start(s8[5242880]{0:T(1024)(128)(4,1)} %bitcast.244), calls=%async_computation.4 | async-start | bytes 8388608
  182.0 17.0 %slice-start.1 = ((s8[5242880]{0:T(1024)(128)(4,1)}), s8[1048576]{0:T(1024)(128)(4,1)S(1)}, s32[]{:S(2)}) async-start(s8[5242880]{0:T(1024)(128)(4,1)} %bitcast.244), calls=%async_computation.5 | async-start | bytes 2097152
  199.0 8.1 %copy-start.3 = (bf16[4,128,2048]{2,1,0:T(8,128)(2,1)}, bf16[4,128,2048]{2,1,0:T(8,128)(2,1)S(1)}, u32[]{:S(2)}) copy-start(bf16[4,128,2048]{2,1,0:T(8,128)(2,1)S(1)} %gather_rows.2) | copy-start | bytes 6291460
  199.0 9.1 %copy-start.13 = (bf16[4,128,2048]{2,1,0:T(8,128)(2,1)S(1)}, bf16[4,128,2048]{2,1,0:T(8,128)(2,1)}, u32[]{:S(2)}) copy-start(bf16[4,128,2048]{2,1,0:T(8,128)(2,1)} %copy-done.12) | copy-start | bytes 6291460
  212.5 8.0 %copy-start.4 = (bf16[4,128,2048]{2,1,0:T(8,128)(2,1)S(1)}, bf16[4,128,2048]{2,1,0:T(8,128)(2,1)}, u32[]{:S(2)}) copy-start(bf16[4,128,2048]{2,1,0:T(8,128)(2,1)} %copy-done.3) | copy-start | bytes 6291460
  252.9 24.0 %copy-start.17 = (f32[128,2048]{1,0:T(8,128)S(1)}, f32[128,2048]{1,0:T(8,128)}, u32[]{:S(2)}) copy-start(f32[128,2048]{1,0:T(8,128)} %copy-done.16) | copy-start | bytes 3145732
  255.7 1.6 copy-start.5
  307.4 6.5 %copy-start.8 = (f32[4,256,128]{2,1,0:T(8,128)S(1)}, f32[4,256,128]{2,1,0:T(8,128)}, u32[]{:S(2)}) copy-start(f32[4,256,128]{2,1,0:T(8,128)} %copy-done.7) | copy-start | bytes 1572868
  307.4 6.5 %copy-start.11 = (bf16[4,4,2,256,128]{4,3,2,1,0:T(8,128)(2,1)S(1)}, bf16[4,4,2,256,128]{4,3,2,1,0:T(8,128)(2,1)}, u32[]{:S(2)}) copy-start(bf16[4,4,2,256,128]{4,3,2,1,0:T(8,128)(2,1)} %copy-done.10) | copy-start | bytes 6291460
  307.4 6.5 %copy-start.15 = (f32[4,256,128]{2,1,0:T(8,128)S(1)}, f32[4,256,128]{2,1,0:T(8,128)}, u32[]{:S(2)}) copy-start(f32[4,256,128]{2,1,0:T(8,128)} %copy-done.14) | copy-start | bytes 1572868
  336.8 43.0 %copy-start.18 = (f32[128,2048]{1,0:T(8,128)S(1)}, f32[128,2048]{1,0:T(8,128)}, u32[]{:S(2)}) copy-start(f32[128,2048]{1,0:T(8,128)} %copy-done.16) | copy-start | bytes 3145732
  393.8 6.2 %copy-start.2 = (bf16[4,128,2048]{2,1,0:T(8,128)(2,1)S(1)}, bf16[4,128,2048]{2,1,0:T(8,128)(2,1)}, u32[]{:S(2)}) copy-start(bf16[4,128,2048]{2,1,0:T(8,128)(2,1)} %copy-done.1) | copy-start | bytes 6291460
  393.8 6.2 %copy-start.26 = (bf16[2,2,256,128]{3,1,2,0:T(2,128)(2,1)S(1)}, bf16[2,2,256,128]{3,1,2,0:T(2,128)(2,1)}, u32[]{:S(2)}) copy-start(bf16[2,2,256,128]{3,1,2,0:T(2,128)(2,1)} %copy.138) | copy-start | bytes 786436
  400.0 1.8 copy-start.27
  406.1 7.1 %copy-start.6 = (bf16[512,2048]{1,0:T(8,128)(2,1)S(1)}, bf16[512,2048]{1,0:T(8,128)(2,1)}, u32[]{:S(2)}) copy-start(bf16[512,2048]{1,0:T(8,128)(2,1)} %get-tuple-element.89) | copy-start | bytes 6291460
  (14 other events, 16.3 us)
Sparse Core Ops, SparseCore 0:
  58.8 69.5 all-gather.2
  130.5 56.1 all-gather.4
  253.0 88.9 reduce-scatter.3

commit v3 on v2

--- a/solution.py
+++ b/solution.py
@@ -18,6 +18,7 @@
 ZY = ("z", "y")
 epsilon = 1e-05
 scale = HD**-0.5
+LOG_BASE = 9.210340371976184
 f32 = jnp.float32
 bf16 = jnp.bfloat16
 
@@ -114,26 +115,6 @@
 def swap_peers():
     d, c = lax.axis_index("dp"), lax.axis_index("c")
     return [{"dp": 1 - d}, {"dp": 1 - d, "c": 1 - c}]
-
-
-def quarter_kernel(count, *refs):
-    srcs, dsts = refs[:count], refs[count : 2 * count]
-    sems = Sems(*refs[2 * count :])
-    greet([tensor_place()[3], *swap_peers()])
-    run(swap_plan(srcs, [lambda me, o=o: o.at[me] for o in dsts], sems))
-
-
-def swap_quarters(collective_id, *arrays):
-    n = len(arrays)
-    return pl.pallas_call(
-        functools.partial(quarter_kernel, n),
-        out_shape=[jax.ShapeDtypeStruct(a.shape, a.dtype) for a in arrays],
-        in_specs=vmem_specs(n),
-        out_specs=vmem_specs(n),
-        scratch_shapes=sem_pair(3 * n),
-        compiler_params=params(collective_id),
-        name="swap_quarters",
-    )(*arrays)
 
 
 CHUNKS = 4
@@ -173,24 +154,6 @@
 ROWS_SEMS = 9
 
 
-def rows_kernel(x, o, send, recv):
-    greet(tensor_place()[3:])
-    run(rows_plan(x, o, Sems(send, recv)))
-
-
-def gather_rows(x):
-    out = pl.pallas_call(
-        rows_kernel,
-        out_shape=jax.ShapeDtypeStruct((4, *x.shape), x.dtype),
-        in_specs=vmem_specs(1),
-        out_specs=vmem_specs(1)[0],
-        scratch_shapes=sem_pair(ROWS_SEMS),
-        compiler_params=params(1),
-        name="gather_rows",
-    )(x)
-    return out.reshape(4 * x.shape[0], x.shape[1])
-
-
 def sum_plan(x, o, buffers, sems):
     from_core, s_here, s_send, from_across, t_send, from_copy = buffers
     d, c, m, core, across, copy_of = tensor_place()
@@ -227,23 +190,6 @@
     pltpu.VMEM((ROWS, D), bf16),
     pltpu.VMEM((ROWS, D), bf16),
 ]
-
-
-def sum_kernel(x, o, *scratch):
-    greet(tensor_place()[3:])
-    run(sum_plan(x, o, scratch[:6], Sems(*scratch[6:])))
-
-
-def sum_rows(x):
-    return pl.pallas_call(
-        sum_kernel,
-        out_shape=jax.ShapeDtypeStruct((ROWS, D), f32),
-        in_specs=vmem_specs(1),
-        out_specs=vmem_specs(1)[0],
-        scratch_shapes=SUM_BUFFERS + sem_pair(SUM_SEMS),
-        compiler_params=params(2),
-        name="sum_rows",
-    )(x.reshape(2, 2, ROWS, D))
 
 
 def weights_plan(w, first, second, low, sems):
@@ -405,30 +351,6 @@
     )(x, cot)
 
 
-def turn_kernel(x, o, send, recv):
-    z, z_up, z_down, z_far, to_z_up, to_z_down = ring("z")
-    peers = [(z_up, to_z_up), (z_down, to_z_down), (z_far, {"z": z_far})]
-    greet([peer for _, peer in peers])
-    sems, copies = Sems(send, recv), []
-    for place, peer in peers:
-        started(copies, x.at[place], o.at[z], *sems.take(), peer)
-    o[z] = x[z]
-    for copy in copies:
-        copy.wait()
-
-
-def turn(x):
-    return pl.pallas_call(
-        turn_kernel,
-        out_shape=jax.ShapeDtypeStruct(x.shape, x.dtype),
-        in_specs=vmem_specs(1),
-        out_specs=vmem_specs(1)[0],
-        scratch_shapes=sem_pair(3),
-        compiler_params=params(5),
-        name="turn",
-    )(x)
-
-
 def ring_sum(at, axis, buffers, sems, put):
     one, two, passed = buffers
     me, up, down, far, to_up, to_down = ring(axis)
@@ -555,19 +477,20 @@
     run(*rings)
 
 
-def end_kernel(wide, g, part, o, gain, summed, *scratch):
+def end_kernel(wide, g, part, feed_part, o, gain, summed, feed_all, *scratch):
     d, c, m, core, across, copy_of = tensor_place()
     _, _, _, _, z_up, z_down = ring("z")
     _, _, _, _, y_up, y_down = ring("y")
     greet([core, across, copy_of, *swap_peers(), z_up, z_down, y_up, y_down])
     shard, mine, theirs, legs_a, legs_b = scratch[:5]
     scratch = scratch[5:]
+    last = Sems(*scratch[18:])
     run(
+        swap_plan([feed_part], [lambda me: feed_all.at[me]], last),
         sum_plan(part, summed, scratch[6:12], Sems(*scratch[12:14])),
         grads_plan(g, shard, "z", "y", 0, legs_a, scratch[:3], Sems(*scratch[14:16])),
         grads_plan(g, shard, "y", "z", 2, legs_b, scratch[3:6], Sems(*scratch[16:18])),
     )
-    last = Sems(*scratch[18:])
     run(swap_plan([shard], [lambda me: o.at[me]], last))
     lanes = pl.ds(wide, HD)
     mine[...] = added(o[0, :, lanes], o[1, :, lanes], o[2, :, lanes], o[3, :, lanes])
@@ -577,7 +500,7 @@
     gain[...] = mine[...] + theirs[...]
 
 
-def end(g, part):
+def end(g, part, feed_part):
     block = (32, g.shape[1])
     return pl.pallas_call(
         functools.partial(end_kernel, g.shape[1] - HD),
@@ -585,9 +508,10 @@
             jax.ShapeDtypeStruct((4, *block), bf16),
             jax.ShapeDtypeStruct((32, HD), f32),
             jax.ShapeDtypeStruct((ROWS, D), f32),
+            jax.ShapeDtypeStruct(feed_part.shape, bf16),
         ],
-        in_specs=vmem_specs(2),
-        out_specs=vmem_specs(3),
+        in_specs=vmem_specs(3),
+        out_specs=vmem_specs(4),
         scratch_shapes=[
             pltpu.VMEM((4, *block), bf16),
             pltpu.VMEM((32, HD), f32),
@@ -601,18 +525,19 @@
         + sem_pair(SUM_SEMS)
         + sem_pair(5 * RING_SEMS)
         + sem_pair(5 * RING_SEMS)
-        + sem_pair(4),
+        + sem_pair(7),
         compiler_params=params(7),
         name="end",
-    )(g.reshape(4, 4, 4, *block), part.reshape(2, 2, ROWS, D))
-
-
-def reach(info, block):
-    t = block * BLOCK + lax.broadcasted_iota(jnp.int32, (BLOCK, 1), 0)
-    begin = jnp.where(t >= info[2], info[2], jnp.where(t >= info[1], info[1], info[0]))
-    end = jnp.minimum((t // FRAME + 1) * FRAME, info[3])
-    living = t < info[3]
-    return jnp.where(living, begin, t), jnp.where(living, end, t + 1)
+    )(g.reshape(4, 4, 4, *block), part.reshape(2, 2, ROWS, D), feed_part)
+
+
+def reach(facts, block, rows):
+    t = block * rows + lax.broadcasted_iota(jnp.int32, (rows, 1), 0)
+    one, two, three, padding = (facts[:, k : k + 1].astype(jnp.int32) for k in range(2, 6))
+    begin = jnp.where(t >= three, three, jnp.where(t >= two, two, one))
+    living = t < LEN - padding
+    end = jnp.minimum((t // FRAME + 1) * FRAME, LEN - padding)
+    return t, begin, jnp.where(living, begin, t), jnp.where(living, end, t + 1)
 
 
 def dot_t(a, b):
@@ -629,9 +554,9 @@
     return jnp.where((at >= low) & (at < high), s, -1e30)
 
 
-def attend_kernel(info, q_ref, kv_ref, o_ref, lse_ref):
-    block = 4 * pl.program_id(0) + info[4]
-    low, high = reach(info, block)
+def attend_kernel(facts, q_ref, kv_ref, o_ref, lse_ref, mixed_ref):
+    block = 4 * pl.program_id(0) + lax.axis_index("y")
+    _, _, low, high = reach(facts[pl.ds(lax.axis_index("z") // 2, 1)], block, BLOCK)
     q = q_ref[0]
 
     def step(j, state):
@@ -650,31 +575,33 @@
         step,
         (jnp.full((BLOCK, 1), -1e30, f32), jnp.zeros((BLOCK, 1), f32), jnp.zeros((BLOCK, HD), f32)),
     )
-    o_ref[0] = acc / total
+    out = acc / total
+    o_ref[0] = out
+    mixed_ref[0] = out.astype(bf16)
     lse_ref[0] = jnp.broadcast_to(top + jnp.log(total), (BLOCK, HD))
 
 
-def attend(info, q, kv):
+def attend(facts, q, kv):
     return pl.pallas_call(
         attend_kernel,
         grid=(4,),
-        out_shape=[jax.ShapeDtypeStruct((4, BLOCK, HD), f32)] * 2,
+        out_shape=[jax.ShapeDtypeStruct((4, BLOCK, HD), f32)] * 2 + [jax.ShapeDtypeStruct((4, BLOCK, HD), bf16)],
         in_specs=[
-            pl.BlockSpec(memory_space=pltpu.SMEM),
+            pl.BlockSpec((8, HD), lambda i: (0, 0)),
             pl.BlockSpec((1, BLOCK, HD), lambda i: (i, 0, 0)),
             pl.BlockSpec((16, 2, BLOCK, HD), lambda i: (0, 0, 0, 0)),
         ],
-        out_specs=[pl.BlockSpec((1, BLOCK, HD), lambda i: (i, 0, 0))] * 2,
+        out_specs=[pl.BlockSpec((1, BLOCK, HD), lambda i: (i, 0, 0))] * 3,
         compiler_params=params(),
         cost_estimate=pl.CostEstimate(flops=20 * 10**9, bytes_accessed=4 * 10**6, transcendentals=10**6),
         name="attend",
-    )(info, q, kv.reshape(16, 2, BLOCK, HD))
-
-
-def attend_back_kernel(info, q_ref, kv_ref, o_ref, lse_ref, do_ref, dq_ref, dkv_ref, acc):
+    )(facts, q, kv.reshape(16, 2, BLOCK, HD))
+
+
+def attend_back_kernel(facts, q_ref, kv_ref, o_ref, lse_ref, do_ref, dq_ref, dkv_ref, acc):
     i = pl.program_id(0)
-    block = 4 * i + info[4]
-    low, high = reach(info, block)
+    block = 4 * i + lax.axis_index("y")
+    _, _, low, high = reach(facts[pl.ds(lax.axis_index("z") // 2, 1)], block, BLOCK)
     q, do = q_ref[0], do_ref[0]
     lse = lse_ref[0][:, :1]
     inner = jnp.sum(o_ref[0] * do.astype(f32), -1, keepdims=True)
@@ -704,7 +631,7 @@
         lax.fori_loop(0, 16, cast, 0)
 
 
-def attend_back(info, q, kv, o, lse, do):
+def attend_back(facts, q, kv, o, lse, do):
     dq, dkv = pl.pallas_call(
         attend_back_kernel,
         grid=(4,),
@@ -713,7 +640,7 @@
             jax.ShapeDtypeStruct((16, 2, BLOCK, HD), bf16),
         ],
         in_specs=[
-            pl.BlockSpec(memory_space=pltpu.SMEM),
+            pl.BlockSpec((8, HD), lambda i: (0, 0)),
             pl.BlockSpec((1, BLOCK, HD), lambda i: (i, 0, 0)),
             pl.BlockSpec((16, 2, BLOCK, HD), lambda i: (0, 0, 0, 0)),
         ]
@@ -726,16 +653,8 @@
         compiler_params=params(),
         cost_estimate=pl.CostEstimate(flops=30 * 10**9, bytes_accessed=8 * 10**6, transcendentals=10**6),
         name="attend_back",
-    )(info, q, kv.reshape(16, 2, BLOCK, HD), o, lse, do)
+    )(facts, q, kv.reshape(16, 2, BLOCK, HD), o, lse, do)
     return dq, dkv.reshape(4, 4, 2, BLOCK, HD)
-
-
-def to_inner(x):
-    return x.reshape(-1, 2, 16, 64).swapaxes(1, 2).reshape(-1, D)
-
-
-def to_outer(x):
-    return x.reshape(-1, 16, 2, 64).swapaxes(1, 2).reshape(-1, D)
 
 
 def norm(value):
@@ -749,9 +668,322 @@
     return r * (e - jnp.mean(e, -1, keepdims=True) - n * jnp.mean(e * n, -1, keepdims=True))
 
 
-def turned(x, cosine, sine, direction):
-    a, b = x[..., :64], x[..., 64:]
-    return jnp.concatenate([a * cosine - direction * b * sine, direction * a * sine + b * cosine], -1)
+def one_hot(rows, places):
+    at = lax.broadcasted_iota(jnp.int32, (rows, HD), 0)
+    lane = lax.broadcasted_iota(jnp.int32, (rows, HD), 1)
+    hot = at < 0
+    for k, place in enumerate(places):
+        hot = hot | ((at == k) & (lane == place))
+    return jnp.where(hot, 1.0, 0.0).astype(bf16)
+
+
+def tables(facts, seq, c):
+    block = (4 * lax.axis_index("z") + lax.axis_index("y")) * 2 + c
+    t, begin, _, _ = reach(facts[seq : seq + 1], block, ROWS)
+    lane = lax.broadcasted_iota(jnp.int32, (1, HD), 1)
+    i = jnp.where(lane < HD // 2, lane, lane - HD // 2).astype(f32)
+    angles = (t - begin).astype(f32) * jnp.exp(i * (-2.0 * LOG_BASE / HD))
+    return jnp.cos(angles), jnp.where(lane < HD // 2, -1.0, 1.0) * jnp.sin(angles)
+
+
+def project_kernel(x, w, n1, qkv, gains, facts):
+    side = w[:, 768:896]
+    gains[...] = dot_t(one_hot(8, (0, 1)), side)
+    facts[...] = jnp.zeros_like(facts)
+    facts[0:1] = side[0:1].astype(f32)
+    facts[1:2] = side[64:65].astype(f32)
+    for seq in range(2):
+        for c in range(2):
+            rows = pl.ds((2 * seq + c) * ROWS, ROWS)
+            n, _ = norm(x[rows].astype(f32))
+            n1[rows] = (n * gains[0:1]).astype(bf16)
+            lin = jnp.dot(n1[rows], w[:, :768], preferred_element_type=f32)
+            cosine, sine = tables(facts, seq, c)
+            for kind in range(3):
+                for h in range(2):
+                    v = lin[:, (2 * kind + h) * HD : (2 * kind + h + 1) * HD]
+                    if kind < 2:
+                        v = v * cosine + pltpu.roll(v, HD // 2, 1) * sine
+                    qkv[2 * seq + h, kind, c * ROWS : (c + 1) * ROWS] = v.astype(bf16)
+
+
+def project(x, w):
+    return pl.pallas_call(
+        project_kernel,
+        out_shape=[
+            jax.ShapeDtypeStruct((512, D), bf16),
+            jax.ShapeDtypeStruct((4, 3, BLOCK, HD), bf16),
+            jax.ShapeDtypeStruct((8, D), f32),
+            jax.ShapeDtypeStruct((8, HD), f32),
+        ],
+        in_specs=vmem_specs(2),
+        out_specs=vmem_specs(4),
+        compiler_params=params(),
+        cost_estimate=pl.CostEstimate(flops=10 * 10**9, bytes_accessed=8 * 10**6, transcendentals=10**5),
+        name="project",
+    )(x, w)
+
+
+def unproject_kernel(grads, w, n1, branch, mixed, gains, facts, gain_two, part, last, lin):
+    for seq in range(2):
+        for c in range(2):
+            rows = pl.ds((2 * seq + c) * ROWS, ROWS)
+            cosine, sine = tables(facts, seq, c)
+            for kind in range(3):
+                for h in range(2):
+                    v = grads[2 * seq + h, kind, c * ROWS : (c + 1) * ROWS]
+                    if kind < 2:
+                        v = v.astype(f32)
+                        v = (v * cosine - pltpu.roll(v, HD // 2, 1) * sine).astype(bf16)
+                    lin[rows, (2 * kind + h) * HD : (2 * kind + h + 1) * HD] = v
+    step = 512
+
+    def body(k, _):
+        some = pl.ds(pl.multiple_of(k * step, step), step)
+        p = dot_t(lin[...], w[some, 0:768])
+        part[:, some] = p.astype(bf16)
+        n = n1[:, some]
+        gain_one = jnp.sum(p * n.astype(f32), 0, keepdims=True) / gains[0:1, some]
+        both = jnp.concatenate([gain_one, gain_two[0:1, some], jnp.zeros((6, step), f32)], 0)
+        last[some, 0:768] = dot_l(n, lin[...]).astype(bf16)
+        last[some, 768:1024] = dot_l(branch[:, some], mixed[...]).astype(bf16)
+        last[some, 1024:1152] = dot_l(both.astype(bf16), one_hot(8, (0, 1))).astype(bf16)
+        return 0
+
+    lax.fori_loop(0, D // step, body, 0)
+
+
+def unproject(grads, w, n1, branch, mixed, gains, facts, gain_two):
+    return pl.pallas_call(
+        unproject_kernel,
+        out_shape=[jax.ShapeDtypeStruct((512, D), bf16), jax.ShapeDtypeStruct((D, 1152), bf16)],
+        in_specs=vmem_specs(8),
+        out_specs=vmem_specs(2),
+        scratch_shapes=[pltpu.VMEM((512, 768), bf16)],
+        compiler_params=params(),
+        cost_estimate=pl.CostEstimate(flops=10 * 10**9, bytes_accessed=8 * 10**6, transcendentals=10**5),
+        name="unproject",
+    )(grads, w, n1, branch, mixed, gains, facts, gain_two)
+
+
+def feed_kernel(n2, cot, up, down, part, fed, grads, n2_t, cot_t, part_sum, fed_sum):
+    j = pl.program_id(0)
+
+    @pl.when(j == 0)
+    def _():
+        def body(k, _):
+            some = pl.ds(pl.multiple_of(k * 512, 512), 512)
+            n2_t[some] = n2[:, some].T
+            cot_t[some] = cot[:, some].T
+            return 0
+
+        lax.fori_loop(0, D // 512, body, 0)
+
+    hidden = jnp.dot(n2[...], up[...], preferred_element_type=f32)
+    half = 0.5 * (1.0 + lax.erf(hidden * 0.5**0.5))
+    slope = half + hidden * jnp.exp(-0.5 * hidden * hidden) * (0.5 / jnp.pi) ** 0.5
+    active = (hidden * half).astype(bf16)
+    grad_active = jnp.dot(cot[...], down[...], preferred_element_type=f32)
+    grad_hidden = (grad_active * slope).astype(bf16)
+    grads[:, :256] = jnp.dot(cot_t[...], active, preferred_element_type=f32).astype(bf16)
+    grads[:, 256:] = jnp.dot(n2_t[...], grad_hidden, preferred_element_type=f32).astype(bf16)
+
+    @pl.when(j == 0)
+    def _():
+        part_sum[...] = dot_t(grad_hidden, up[...])
+        fed_sum[...] = dot_t(active, down[...])
+
+    @pl.when(j > 0)
+    def _():
+        part_sum[...] += dot_t(grad_hidden, up[...])
+        fed_sum[...] += dot_t(active, down[...])
+
+    @pl.when(j == 3)
+    def _():
+        part[...] = part_sum[...].astype(bf16)
+        fed[...] = fed_sum[...].astype(bf16)
+
+
+def feed(n2, cot, second, down):
+    whole = pl.BlockSpec((512, D), lambda j: (0, 0))
+    return pl.pallas_call(
+        feed_kernel,
+        grid=(4,),
+        out_shape=[jax.ShapeDtypeStruct((512, D), bf16)] * 2 + [jax.ShapeDtypeStruct((D, 2048), bf16)],
+        in_specs=[
+            whole,
+            whole,
+            pl.BlockSpec((D, 256), lambda j: (0, j + 1)),
+            pl.BlockSpec((D, 256), lambda j: (0, j)),
+        ],
+        out_specs=[whole, whole, pl.BlockSpec((D, 512), lambda j: (0, j))],
+        scratch_shapes=[pltpu.VMEM((D, 512), bf16)] * 2 + [pltpu.VMEM((512, D), f32)] * 2,
+        compiler_params=params(vmem=56),
+        cost_estimate=pl.CostEstimate(flops=20 * 10**9, bytes_accessed=24 * 10**6, transcendentals=10**6),
+        name="feed",
+    )(n2, cot, second, down)
+
+
+def sum_norm_plan(x, own, all_rows, make, buffers, sems):
+    from_core, s_here, s_send, from_across, t_send, from_copy = buffers
+    d, c, m, core, across, copy_of = tensor_place()
+    me, far = 2 * d + c, 2 * (1 - d) + c
+    step = ROWS // CHUNKS
+    rows = [pl.ds(k * step, step) for k in range(CHUNKS)]
+    copies, zero, one, two = [], [], [], []
+    for r in rows:
+        zero.append(started(copies, x.at[:, 1 - c, r], from_core.at[:, r], *sems.take(), core))
+    yield
+    for k, r in enumerate(rows):
+        zero[k].wait_recv()
+        s_send[r] = added(x[1 - d, c, r], from_core[1 - d, r]).astype(bf16)
+        one.append(started(copies, s_send.at[r], from_across.at[r], *sems.take(), across))
+        s_here[r] = added(x[d, c, r], from_core[d, r])
+    for k, r in enumerate(rows):
+        one[k].wait_recv()
+        t_send[r] = added(s_here[r], from_across[r]).astype(bf16)
+        two.append(started(copies, t_send.at[r], from_copy.at[r], *sems.take(), copy_of))
+    yield
+    nears, firsts, seconds, lasts = [], [], [], []
+    for k, r in enumerate(rows):
+        two[k].wait_recv()
+        all_rows[me, r] = make(r, added(t_send[r], from_copy[r])).astype(bf16)
+        nears.append(started(copies, all_rows.at[me, r], all_rows.at[me, r], *sems.take(), core))
+        half = pl.ds(pl.multiple_of(k * step + m * (step // 2), step // 2), step // 2)
+        firsts.append(started(copies, all_rows.at[me, half], all_rows.at[me, half], *sems.take(), across))
+    yield
+
+    def onward(half, peer):
+        return started(copies, all_rows.at[far, half], all_rows.at[far, half], *sems.take(), peer)
+
+    for k in range(CHUNKS):
+        firsts[k].wait_recv()
+        half = pl.ds(pl.multiple_of(k * step + (1 - m) * (step // 2), step // 2), step // 2)
+        seconds.append(onward(half, copy_of))
+        lasts.append(onward(half, core))
+    yield
+    for k in range(CHUNKS):
+        seconds[k].wait_recv()
+        half = pl.ds(pl.multiple_of(k * step + m * (step // 2), step // 2), step // 2)
+        lasts.append(onward(half, core))
+    yield
+    for copy in nears + lasts:
+        copy.wait_recv()
+    yield
+    for copy in copies:
+        copy.wait_send()
+
+
+SUM_NORM_SEMS = 8 * CHUNKS
+
+
+def z_peers():
+    z, z_up, z_down, z_far, to_z_up, to_z_down = ring("z")
+    return z, [(z_up, to_z_up), (z_down, to_z_down), (z_far, {"z": z_far})]
+
+
+def mix_kernel(o, w, x, gains, mixed, middle, n2, turned, part, *scratch):
+    z, peers = z_peers()
+    c = lax.axis_index("c")
+    greet([*tensor_place()[3:], *[peer for _, peer in peers]])
+    turns, copies = Sems(*scratch[8:]), []
+    for place, peer in peers:
+        started(copies, o.at[place], turned.at[z], *turns.take(), peer)
+    turned[z] = o[z]
+    for copy in copies:
+        copy.wait()
+    for seq in range(2):
+        for h in range(2):
+            mixed[seq * BLOCK : (seq + 1) * BLOCK, h * HD : (h + 1) * HD] = turned[2 * seq + h]
+
+    def partial(to):
+        for seq in range(2):
+            rows = pl.ds(pl.multiple_of(seq * BLOCK + to * ROWS, ROWS), ROWS)
+            part[seq, to] = dot_t(mixed[rows], w[...]).astype(bf16)
+
+    def make(r, total):
+        value = x[r].astype(f32) + total
+        middle[r] = value
+        return norm(value)[0] * gains[1:2]
+
+    partial(1 - c)
+    plan = sum_norm_plan(part, middle, n2, make, scratch[:6], Sems(*scratch[6:8]))
+    next(plan)
+    partial(c)
+    run(plan)
+
+
+def mix(o, second, x, gains):
+    whole = lambda *shape: pl.BlockSpec(shape, lambda i: (0,) * len(shape))
+    return pl.pallas_call(
+        mix_kernel,
+        grid=(1,),
+        out_shape=[
+            jax.ShapeDtypeStruct((512, 256), bf16),
+            jax.ShapeDtypeStruct((ROWS, D), f32),
+            jax.ShapeDtypeStruct((4, ROWS, D), bf16),
+        ],
+        in_specs=[whole(4, BLOCK, HD), whole(D, 256), whole(ROWS, D), whole(8, D)],
+        out_specs=[whole(512, 256), whole(ROWS, D), whole(4, ROWS, D)],
+        scratch_shapes=[pltpu.VMEM((4, BLOCK, HD), bf16), pltpu.VMEM((2, 2, ROWS, D), bf16)]
+        + SUM_BUFFERS
+        + sem_pair(SUM_NORM_SEMS)
+        + sem_pair(3),
+        compiler_params=params(1),
+        name="mix",
+    )(o, second, x, gains)
+
+
+def unmix_kernel(part, middle, cot, gains, w, grad_middle, branch, turned, gain_two, grad_mixed, *scratch):
+    z, peers = z_peers()
+    greet([*tensor_place()[3:], *[peer for _, peer in peers]])
+    gain_two[...] = jnp.zeros_like(gain_two)
+
+    def make(r, total):
+        n, rate = norm(middle[r])
+        gain_two[0:1] += 0.5 * jnp.sum(total * n, 0, keepdims=True)
+        value = cot[r].astype(f32) + norm_back(total, n, rate, gains[1:2])
+        grad_middle[r] = value
+        return value
+
+    run(sum_norm_plan(part, grad_middle, branch, make, scratch[:6], Sems(*scratch[6:8])))
+    for k in range(4):
+        value = jnp.dot(branch[k], w[...], preferred_element_type=f32).astype(bf16)
+        for h in range(2):
+            grad_mixed[2 * (k // 2) + h, (k % 2) * ROWS : (k % 2 + 1) * ROWS] = value[:, h * HD : (h + 1) * HD]
+    turns, copies = Sems(*scratch[8:]), []
+    for place, peer in peers:
+        started(copies, grad_mixed.at[place], turned.at[z], *turns.take(), peer)
+    turned[z] = grad_mixed[z]
+    for copy in copies:
+        copy.wait()
+
+
+def unmix(part, middle, cot, gains, second):
+    whole = lambda *shape: pl.BlockSpec(shape, lambda i: (0,) * len(shape))
+    return pl.pallas_call(
+        unmix_kernel,
+        grid=(1,),
+        out_shape=[
+            jax.ShapeDtypeStruct((ROWS, D), f32),
+            jax.ShapeDtypeStruct((4, ROWS, D), bf16),
+            jax.ShapeDtypeStruct((4, BLOCK, HD), bf16),
+            jax.ShapeDtypeStruct((8, D), f32),
+        ],
+        in_specs=[whole(2, 2, ROWS, D), whole(ROWS, D), whole(ROWS, D), whole(8, D), whole(D, 256)],
+        out_specs=[whole(ROWS, D), whole(4, ROWS, D), whole(4, BLOCK, HD), whole(8, D)],
+        scratch_shapes=[pltpu.VMEM((4, BLOCK, HD), bf16)] + SUM_BUFFERS + sem_pair(SUM_NORM_SEMS) + sem_pair(3),
+        compiler_params=params(2),
+        name="unmix",
+    )(part.reshape(2, 2, ROWS, D), middle, cot, gains, second)
+
+
+def to_inner(x):
+    return x.reshape(-1, 2, 16, 64).swapaxes(1, 2).reshape(-1, D)
+
+
+def to_outer(x):
+    return x.reshape(-1, 16, 2, 64).swapaxes(1, 2).reshape(-1, D)
 
 
 def quarters(w):
@@ -760,10 +992,6 @@
 
 def joined(w):
     return w.swapaxes(0, 1).reshape(w.shape[1], -1)
-
-
-def gelu(v):
-    return jax.nn.gelu(v, approximate=False)
 
 
 def gather_weights(x):
@@ -788,8 +1016,6 @@
     gain_second,
     cotangent,
 ):
-    z, y = lax.axis_index("z"), lax.axis_index("y")
-    living = LEN - pad_lengths
     side = jnp.concatenate(
         [
             gain_first[:, None],
@@ -811,83 +1037,23 @@
     second = gather_weights(second.reshape(HD, -1))
     down = gather_weights(third.reshape(HD, -1))
 
-    side = first[:, 768:]
-    gains = side[:, :2].astype(f32).T
-    gain_one, gain_two = gains[0], gains[1]
-    facts = side[:128:64, 2:6].astype(jnp.int32)
-    begins, ends = facts[:, :3], LEN - facts[:, 3]
-
-    n_all, _ = norm(x_all.reshape(512, D).astype(f32))
-    normed_one = (n_all * gain_one).astype(bf16)
     incoming = to_inner(cotangent[0])
-
-    places = (4 * z + y) * BLOCK + jnp.arange(BLOCK, dtype=jnp.int32)
-    opened = begins[:, None, :] <= places[None, :, None]
-    position = places - jnp.max(jnp.where(opened, begins[:, None, :], 0), -1)
-    frequency = 10000.0 ** (-2.0 * jnp.arange(HD // 2, dtype=f32) / HD)
-    angles = position.astype(f32)[..., None] * frequency
-    cosine, sine = jnp.cos(angles)[:, :, None], jnp.sin(angles)[:, :, None]
-
-    lin = jnp.dot(normed_one, first, preferred_element_type=f32)
-    lin = lin[:, :768].reshape(2, BLOCK, 3, 2, HD)
-    query = turned(lin[:, :, 0], cosine, sine, 1.0)
-    key = turned(lin[:, :, 1], cosine, sine, 1.0)
-    qkv = jnp.stack([query, key, lin[:, :, 2]], 0).astype(bf16)
-    qkv = qkv.transpose(1, 3, 0, 2, 4).reshape(4, 3, BLOCK, HD)
+    normed_one, qkv, gains, facts = project(x_all.reshape(512, D), first)
     q, kv, incoming_all = spread(qkv, incoming)
     incoming_all = incoming_all.reshape(512, D)
-    mine = z // 2
-    info = jnp.concatenate(
-        [lax.dynamic_index_in_dim(begins, mine, 0, False), lax.dynamic_index_in_dim(ends, mine, 0), y[None]]
-    ).astype(jnp.int32)
-    o, lse = attend(info, q, kv)
-    mixed = turn(o.astype(bf16))
-    mixed = mixed.reshape(2, 2, BLOCK, HD).swapaxes(1, 2).reshape(512, 2 * HD)
-
-    x = x_here.astype(f32)
-    out = second[:, :256]
-    middle = x + sum_rows(dot_t(mixed, out).astype(bf16))
-    n_two, r_two = norm(middle)
-    normed_two = gather_rows((n_two * gain_two).astype(bf16))
-    hidden = jnp.dot(normed_two, second, preferred_element_type=f32)[:, 256:]
-    active, pull = jax.vjp(gelu, hidden)
-    active = active.astype(bf16)
-    grad_active = jnp.dot(incoming_all, down, preferred_element_type=f32)
-    grad_hidden = pull(grad_active)[0].astype(bf16)
-    part_two = dot_t(jnp.pad(grad_hidden, ((0, 0), (256, 0))), second).astype(bf16)
-    feed = jnp.concatenate(
-        [dot_l(incoming_all, active).astype(bf16), dot_l(normed_two, grad_hidden).astype(bf16)], 1
-    )
-    part_two, feed = lax.optimization_barrier((part_two, feed))
-    feed = scatter_grads(feed)
-    grad_normed_two = sum_rows(part_two)
-    grad_middle = incoming.astype(f32) + norm_back(grad_normed_two, n_two, r_two, gain_two)
-    branch = gather_rows(grad_middle.astype(bf16))
-
-    grad_mixed = jnp.dot(branch, out, preferred_element_type=f32).astype(bf16)
-    grad_mixed = grad_mixed.reshape(2, BLOCK, 2, HD).swapaxes(1, 2).reshape(4, BLOCK, HD)
-    dq, dkv = attend_back(info, q, kv, o, lse, turn(grad_mixed))
-    grads, fed = collect(dq, dkv, dot_t(active, down).astype(bf16))
+    o, lse, attended = attend(facts, q, kv)
+    mixed, middle, normed_two = mix(attended, second, x_here, gains)
+    part_two, part_out, grad_feed = feed(normed_two.reshape(512, D), incoming_all, second, down)
+    grad_feed = scatter_grads(grad_feed)
+    grad_middle, branch, grad_mixed, gain_two = unmix(part_two, middle, incoming, gains, second)
+    dq, dkv = attend_back(facts, q, kv, o, lse, grad_mixed)
+    grads, fed = collect(dq, dkv, part_out)
     output = middle + fed
-    grads = grads.reshape(2, 2, 3, BLOCK, HD).transpose(2, 0, 3, 1, 4)
-    grad_query = turned(grads[0].astype(f32), cosine, sine, -1.0).astype(bf16)
-    grad_key = turned(grads[1].astype(f32), cosine, sine, -1.0).astype(bf16)
-    grad_lin = jnp.stack([grad_query, grad_key, grads[2]], 2).reshape(512, 768)
-
-    part_one = dot_t(jnp.pad(grad_lin, ((0, 0), (0, HD))), first)
-    gain_grads = jnp.stack([jnp.sum(part_one * n_all, 0), 0.5 * jnp.sum(grad_normed_two * n_two, 0)], 1)
-    last = jnp.concatenate(
-        [
-            dot_l(normed_one, grad_lin).astype(bf16),
-            dot_l(branch, mixed).astype(bf16),
-            jnp.pad(gain_grads, ((0, 0), (0, HD - 2))).astype(bf16),
-        ],
-        1,
-    )
-    last, gain_grads, grad_normed_one = end(last, part_one.astype(bf16))
-    n_one, r_one = norm(x)
-    grad_input = grad_middle + norm_back(grad_normed_one, n_one, r_one, gain_one)
-    feed = swap_quarters(8, feed.reshape(4, 32, -1))[0].astype(f32)
+    part_one, last = unproject(grads, first, normed_one, branch.reshape(512, D), mixed, gains, facts, gain_two)
+    last, gain_grads, grad_normed_one, grad_feed = end(last, part_one, grad_feed.reshape(4, 32, -1))
+    n_one, r_one = norm(x_here.astype(f32))
+    grad_input = grad_middle + norm_back(grad_normed_one, n_one, r_one, gains[0])
+    grad_feed = grad_feed.reshape(4, 32, 4, 2, 256).transpose(3, 1, 0, 2, 4).reshape(2, 32, -1).astype(f32)
     last = last.astype(f32)
     return (
         to_outer(output).astype(bf16)[None],
@@ -896,8 +1062,8 @@
         joined(last[:, :, 256:512]),
         joined(last[:, :, 512:768]),
         joined(last[:, :, 768:1024]).T,
-        joined(feed[:, :, 1024:]),
-        joined(feed[:, :, :1024]).T,
+        grad_feed[1],
+        grad_feed[0].T,
         gain_grads[:, 0],
         gain_grads[:, 1],
     )

time: 493 us -> 387 us (0.78); the launches traced: 487 us -> 386 us
  matrix products: 53 us -> 0 us
  local copies, waits for them, and re-layouts: 72.9 us -> 34.9 us
  other arithmetic: 34.7 us -> 2.81 us
  waiting for transfers between devices: 0.73 us -> 18.7 us
  Pallas kernels: 310 us -> 315 us
    dot_general x12 -> x0, matrix products: 53 us -> none  [the longest x4 21.7 us: dot_t(): lax.dot_general(a, b, (((1,), (1,)), ((), ())), preferred_element_type=f32)]
    pallas_call x7 -> x5, Pallas kernels: 103 us -> 124 us  [the longest x1 44.4 us: unmix(): pl.pallas_call(unmix_kernel, grid=(1,), out_shape=[jax.ShapeDtypeStruct((...]
    all_gather x2, waiting for transfers between devices: 0.01 us -> 18 us  [gather_weights(): return lax.all_gather(x, ZY, axis=0, tiled=True)]
    unnamed x80 -> x49, local copies, waits for them, and re-layouts: 35.9 us -> 20.8 us
    concatenate x6 -> x0, other arithmetic: 14.8 us -> none  [the longest x1 8.35 us: local(): jnp.concatenate([dot_l(incoming_all, active).astype(bf16), dot_l(normed_t...]
    pallas_call x1, Pallas kernels: 37.8 us -> 24.6 us  [spread(): pl.pallas_call(spread_kernel, out_shape=[jax.ShapeDtypeStruct((4, BLOCK,...]
    concatenate x1 -> x0, local copies, waits for them, and re-layouts: 7.13 us -> none  [local(): jnp.concatenate([dot_l(normed_one, grad_lin).astype(bf16), dot_l(branch,...]
    reshape x6 -> x0, local copies, waits for them, and re-layouts: 6.54 us -> none  [the longest x1 3.43 us: local(): lin = lin[:, :768].reshape(2, BLOCK, 3, 2, HD)]
  transfers between devices with their start and end apart: 3 -> 3, of which waited for: 0 -> 2; matrix products, arithmetic and copies ran while one was open for 20% -> 1% of each run, Pallas kernels for 53% -> 52%
where the time goes in v3:
time: 387 us; the launch traced here: 386 us
  Pallas kernels  315 us (81%)
  local copies, waits for them, and re-layouts  34.9 us (9%)
  waiting for transfers between devices  18.7 us (5%)
  between operations  14.8 us (4%)
    pallas_call x1, Pallas kernels, end(): pl.pallas_call(functools.partial(end_kernel, g.shape[1] - HD), out_shape=...  47.1 us
    pallas_call x1, Pallas kernels, unmix(): pl.pallas_call(unmix_kernel, grid=(1,), out_shape=[jax.ShapeDtypeStruct((...  44.4 us
    pallas_call x1, Pallas kernels, start(): pl.pallas_call(start_kernel, out_shape=[jax.ShapeDtypeStruct((4, 4, *firs...  42.8 us
    pallas_call x1, Pallas kernels, mix(): pl.pallas_call(mix_kernel, grid=(1,), out_shape=[jax.ShapeDtypeStruct((51...  40.3 us
    pallas_call x1, Pallas kernels, collect(): pl.pallas_call(collect_kernel, out_shape=[jax.ShapeDtypeStruct((4, 3, BLO...  37.5 us
    pallas_call x1, Pallas kernels, spread(): pl.pallas_call(spread_kernel, out_shape=[jax.ShapeDtypeStruct((4, BLOCK,...  24.6 us
    pallas_call x1, Pallas kernels, attend_back(): pl.pallas_call(attend_back_kernel, grid=(4,), out_shape=[jax.ShapeDtypeSt...  22.6 us
    pallas_call x1, Pallas kernels, feed(): pl.pallas_call(feed_kernel, grid=(4,), out_shape=[jax.ShapeDtypeStruct((5...  22.6 us
  transfers between devices with their start and end apart: 3, of which 2 were waited for; matrix products, arithmetic and copies ran while one was open for 1% of the time, Pallas kernels for 52%

profile of v3, /device:TPU:1, one launch (start us, length us, event | category | flops | bytes accessed | tf_op | source)
XLA Modules:
  0.0 386.2 jit_solution(5040547600749665474)
XLA Ops:
  13.7 1.3 copy.38
  16.3 42.8 %start.1 = (bf16[4,4,4,32,896]{4,3,2,1,0:T(8,128)(2,1)}, bf16[4,32,1280]{2,1,0:T(8,128)(2,1)}, bf16[4,32,1024]{2,1,0:T(8,128)(2,1)}, bf16[4,128,2048]{2,1,0:T(8,128)(2,1)S(1)}) custom-call(bf16[4,32,896]{2,1,0:T(8,128)(2,1)S(1)} %pad_maximum_fusion.1.first, bf16[4,32,1280]{2,1,0:T(8,128)(2,1)S(1)} %pad_maximum_fusion.second, ...), custom_call_target="tpu_custom_call" | custom-call | tf_op jit(solution)/shard_map/start/pallas_call | solution.py:269
  59.1 1.3 copy-done.6
  61.8 1.6 copy-done.7
  63.4 5.4 %project.1 = (bf16[512,2048]{1,0:T(8,128)(2,1)S(1)}, bf16[4,3,256,128]{3,2,1,0:T(8,128)(2,1)S(1)}, f32[8,2048]{1,0:T(8,128)S(1)}, f32[8,128]{1,0:T(8,128)S(1)}) custom-call(bf16[512,2048]{1,0:T(8,128)(2,1)S(1)} %bitcast.103, bf16[2048,896]{1,0:T(8,128)(2,1)} %bitcast.138), custom_call_target="tpu_custom_call" | custom-call | flops 10000000000 | bytes 8000000 | tf_op jit(solution)/shard_map/project/pallas_call | solution.py:711
  68.9 1.3 copy-done.12
  70.2 24.6 %spread.1 = (bf16[4,256,128]{2,1,0:T(8,128)(2,1)S(1)}, bf16[4,4,2,256,128]{4,3,2,1,0:T(8,128)(2,1)S(1)}, bf16[4,128,2048]{2,1,0:T(8,128)(2,1)S(1)}) custom-call(bf16[4,3,256,128]{3,2,1,0:T(8,128)(2,1)S(1)} %get-tuple-element.47.x, bf16[128,2048]{1,0:T(8,128)(2,1)S(1)} %copy.43.cot), custom_call_target="tpu_custom_call" | custom-call | tf_op jit(solution)/shard_map/spread/pallas_call | solution.py:339
  94.8 1.3 copy-done.8
  96.1 16.0 %attend.1 = (f32[4,256,128]{2,1,0:T(8,128)S(1)}, f32[4,256,128]{2,1,0:T(8,128)S(1)}, bf16[4,256,128]{2,1,0:T(8,128)(2,1)S(1)}) custom-call(f32[8,128]{1,0:T(8,128)S(1)} %get-tuple-element.46.facts, bf16[4,256,128]{2,1,0:T(8,128)(2,1)S(1)} %get-tuple-element.48.q_ref, bf16[16,2,256,128]{3,2,1,0:T(8,128)(2,1)S(1)} %bitcast.100), custom_call_target="tpu_custom_call" | custom-call | flops 20000000000 | bytes 4000000 | tf_op jit(solution)/shard_map/attend/pallas_call | solution.py:585
  112.1 1.4 copy-done.3
  114.2 6.1 %all-gather.3.cloned.1.call-done.w.up = bf16[2048,1280]{1,0:T(8,128)(2,1)} async-done(((bf16[128,1280]{1,0:T(8,128)(2,1)}), bf16[2048,1280]{1,0:T(8,128)(2,1)}) %all-gather.3.cloned.1.call-update) | async-done | bytes 5242896 | tf_op jit(solution)/shard_map/all_gather | solution.py:998
  120.3 40.3 %mix.1 = (bf16[512,256]{1,0:T(8,128)(2,1)S(1)}, f32[128,2048]{1,0:T(8,128)S(1)}, bf16[4,128,2048]{2,1,0:T(8,128)(2,1)S(1)}) custom-call(bf16[4,256,128]{2,1,0:T(8,128)(2,1)S(1)} %get-tuple-element.50.o, bf16[2048,1280]{1,0:T(8,128)(2,1)} %all-gather.3.cloned.1.call-done.w.up, bf16[128,2048]{1,0:T(8,128)(2,1)S(1)} %copy.40.x, ...), custom_call_target="tpu_custom_call" | custom-call | tf_op jit(solution)/shard_map/mix/pallas_call | solution.py:918
  160.6 1.3 copy-done.9
  161.9 11.9 %all-gather.5.cloned.1.call-done.down = bf16[2048,1024]{1,0:T(8,128)(2,1)} async-done(((bf16[128,1024]{1,0:T(8,128)(2,1)}), bf16[2048,1024]{1,0:T(8,128)(2,1)}) %all-gather.5.cloned.1.call-update) | async-done | bytes 4194320 | tf_op jit(solution)/shard_map/all_gather | solution.py:998
  173.8 22.6 %feed.1 = (bf16[512,2048]{1,0:T(8,128)(2,1)}, bf16[512,2048]{1,0:T(8,128)(2,1)}, bf16[2048,2048]{1,0:T(8,128)(2,1)}) custom-call(bf16[512,2048]{1,0:T(8,128)(2,1)} %bitcast.105, bf16[512,2048]{1,0:T(8,128)(2,1)} %bitcast.104, bf16[2048,1280]{1,0:T(8,128)(2,1)} %all-gather.3.cloned.1.call-done.w.up, bf16[2048,1024]{1,0:T(8,128)(2,1)} %all-gather.5.cloned.1.call-done.down), custom_call_target="tpu_custom_call" | custom-call | flops 20000000000 | bytes 24000000 | tf_op jit(solution)/shard_map/feed/pallas_call | solution.py:809
  198.5 44.4 %unmix.1 = (f32[128,2048]{1,0:T(8,128)S(1)}, bf16[4,128,2048]{2,1,0:T(8,128)(2,1)S(1)}, bf16[4,256,128]{2,1,0:T(8,128)(2,1)S(1)}, f32[8,2048]{1,0:T(8,128)S(1)}) custom-call(bf16[2,2,128,2048]{3,2,1,0:T(8,128)(2,1)} %bitcast.113, f32[128,2048]{1,0:T(8,128)S(1)} %get-tuple-element.53.middle, bf16[128,2048]{1,0:T(8,128)(2,1)S(1)} %copy.43.cot, ...), custom_call_target="tpu_custom_call" | custom-call | tf_op jit(solution)/shard_map/unmix/pallas_call | solution.py:964
  243.9 1.3 copy-done.5
  245.2 22.6 %attend_back.1 = (bf16[4,256,128]{2,1,0:T(8,128)(2,1)S(1)}, bf16[16,2,256,128]{3,2,1,0:T(8,128)(2,1)S(1)}) custom-call(f32[8,128]{1,0:T(8,128)S(1)} %get-tuple-element.46.facts, bf16[4,256,128]{2,1,0:T(8,128)(2,1)S(1)} %get-tuple-element.48.q_ref, bf16[16,2,256,128]{3,2,1,0:T(8,128)(2,1)S(1)} %bitcast.101, f32[4,256,128]{2,1,0:T(8,128)S(1)} %get-tuple-element.54.o_ref, ...), custom_call_target="tpu_custom_call" | custom-call | flops 30000001024 | bytes 8000000 | tf_op jit(solution)/shard_map/attend_back/pallas_call | solution.py:635
  267.8 37.5 %collect.1 = (bf16[4,3,256,128]{3,2,1,0:T(8,128)(2,1)S(1)}, f32[128,2048]{1,0:T(8,128)S(1)}) custom-call(bf16[4,256,128]{2,1,0:T(8,128)(2,1)S(1)} %get-tuple-element.61.dq, bf16[4,4,2,256,128]{4,3,2,1,0:T(8,128)(2,1)S(1)} %bitcast.97, bf16[2,2,128,2048]{3,2,1,0:T(8,128)(2,1)} %bitcast.114), custom_call_target="tpu_custom_call" | custom-call | tf_op jit(solution)/shard_map/collect/pallas_call | solution.py:435
  307.7 1.6 copy-done.13
  309.3 11.6 %unproject.1 = (bf16[512,2048]{1,0:T(8,128)(2,1)S(1)}, bf16[2048,1152]{1,0:T(8,128)(2,1)}) custom-call(bf16[4,3,256,128]{3,2,1,0:T(8,128)(2,1)S(1)} %get-tuple-element.66.grads, bf16[2048,896]{1,0:T(8,128)(2,1)} %bitcast.139, bf16[512,2048]{1,0:T(8,128)(2,1)S(1)} %copy-done.13, bf16[512,2048]{1,0:T(8,128)(2,1)} %bitcast.102, ...), custom_call_target="tpu_custom_call" | custom-call | flops 10000000000 | bytes 8000000 | tf_op jit(solution)/shard_map/unproject/pallas_call | solution.py:757
  321.9 47.1 %end.1 = (bf16[4,32,1152]{2,1,0:T(8,128)(2,1)S(1)}, f32[32,128]{1,0:T(8,128)S(1)}, f32[128,2048]{1,0:T(8,128)S(1)}, bf16[4,32,2048]{2,1,0:T(8,128)(2,1)S(1)}) custom-call(bf16[4,4,4,32,1152]{4,3,2,1,0:T(8,128)(2,1)} %bitcast.109, bf16[2,2,128,2048]{3,2,1,0:T(8,128)(2,1)S(1)} %bitcast.96, bf16[4,32,2048]{2,1,0:T(8,128)(2,1)S(1)} %bitcast.99), custom_call_target="tpu_custom_call" | custom-call | tf_op jit(solution)/shard_map/end/pallas_call | solution.py:505
  371.3 1.3 copy.58
  378.6 1.1 squeeze.12
  (90 shorter events, 23.7 us)
Async XLA Ops:
  7.2 113.2 %all-gather.3.cloned.1.call-start = ((), (), s32[]{:S(2)}) async-start(), calls=%async_computation.1 | async-start | bytes 5570560 | tf_op jit(solution)/shard_map/all_gather | solution.py:998
  11.7 4.3 %copy-start.19 = (bf16[32,1024]{1,0:T(8,128)(2,1)S(1)}, bf16[32,1024]{1,0:T(8,128)(2,1)}, u32[]{:S(2)}) copy-start(bf16[32,1024]{1,0:T(8,128)(2,1)} %param.17) | copy-start | bytes 196612
  11.7 4.3 %copy-start.20 = (bf16[32,1024]{1,0:T(8,128)(2,1)S(1)}, bf16[32,1024]{1,0:T(8,128)(2,1)}, u32[]{:S(2)}) copy-start(bf16[32,1024]{1,0:T(8,128)(2,1)} %param.16) | copy-start | bytes 196612
  15.0 0.8 copy-start.16
  15.8 45.4 %copy-start.18 = (bf16[1,128,2048]{2,1,0:T(8,128)(2,1)S(1)}, bf16[1,128,2048]{2,1,0:T(8,128)(2,1)}, u32[]{:S(2)}) copy-start(bf16[1,128,2048]{2,1,0:T(8,128)(2,1)} %param.23) | copy-start | bytes 1572868
  59.1 1.3 copy-start.6
  60.5 113.3 %all-gather.5.cloned.1.call-start = ((), (), s32[]{:S(2)}) async-start(), calls=%async_computation.2 | async-start | bytes 4456448 | tf_op jit(solution)/shard_map/all_gather | solution.py:998
  61.2 259.7 %reduce-scatter.2.cloned.1.call-start = ((), (), s32[]{:S(2)}) async-start(), calls=%async_computation.3 | async-start | bytes 8912896 | tf_op jit(solution)/shard_map/reduce_scatter | solution.py:1002
  61.8 1.6 copy-start.7
  68.9 1.3 copy-start.12
  94.8 1.3 copy-start.8
  112.1 1.4 copy-start.3
  160.6 1.3 copy-start.9
  161.9 34.4 %copy-start.10 = (bf16[512,256]{1,0:T(8,128)(2,1)}, bf16[512,256]{1,0:T(8,128)(2,1)S(1)}, u32[]{:S(2)}) copy-start(bf16[512,256]{1,0:T(8,128)(2,1)S(1)} %get-tuple-element.69.mixed) | copy-start | bytes 786436
  196.4 1.0 copy-start.17
  198.5 46.7 %copy-start.4 = (bf16[4,4,2,256,128]{4,3,2,1,0:T(8,128)(2,1)S(1)}, bf16[4,4,2,256,128]{4,3,2,1,0:T(8,128)(2,1)}, u32[]{:S(2)}) copy-start(bf16[4,4,2,256,128]{4,3,2,1,0:T(8,128)(2,1)} %copy-done.3) | copy-start | bytes 6291460
  198.5 46.7 %copy-start.15 = (f32[4,256,128]{2,1,0:T(8,128)S(1)}, f32[4,256,128]{2,1,0:T(8,128)}, u32[]{:S(2)}) copy-start(f32[4,256,128]{2,1,0:T(8,128)} %copy-done.14) | copy-start | bytes 1572868
  242.9 1.0 copy-start
  243.9 1.3 copy-start.5
  306.7 0.9 copy-start.11
  307.7 1.6 copy-start.13
  320.9 1.0 copy-start.2
  321.9 47.9 %copy-start.21 = (f32[128]{0:T(128)S(1)}, f32[128]{0:T(128)}, u32[]{:S(2)}) copy-start(f32[128]{0:T(128)} %add_rsqrt_fusion) | copy-start | bytes 1540
  369.1 1.2 copy-start.1
  (1 other events, 0.8 us)
Sparse Core Ops, SparseCore 0:
  60.6 59.7 all-gather.2
  122.5 51.2 all-gather.4
  196.5 85.1 reduce-scatter.1
